TPU v7x, 128 devices: a whole 4x4x4 slice. The times are simulated.
128 devices in a mesh: ang: 16 (over x_lo, y, core), slab: 8 (over z, x_hi).
Axes of the slice: x: 4 (x_hi: 2, x_lo: 2; x = x_hi * 2 + x_lo), y: 4, z: 4, core: 2. Of those that a mesh axis runs over, the one named last changes fastest.
Arguments:
- object_field: bfloat16 [2, 8, 1024, 1024], P(None, 'slab'), may hold values from -2 to 2
- probe_field: float32 [2, 256, 256], replicated, may hold values from -6 to 6
- diffraction: float32 [16, 8, 8, 256, 256], P('ang', 'slab'), may hold values from 0.1 to 3
- scan_offsets: int32 [16, 8, 8, 2], P('ang', 'slab'), may hold values from 0 to 768
- counts: int32 [8, 16], P('slab', 'ang'), may hold values from 1 to 8, 64 in all within a row
- band_weights: bfloat16 [16, 8, 2, 4], P(None, 'slab'), may hold values from 0.049804688 to 0.44921875
- band_offsets: int32 [16, 8, 2], P(None, 'slab'), may hold values from -64 to 64
Outputs:
- object_grad: float32 [1024, 2, 8, 1024], P('ang', None, 'slab')
- probe_grad: float32 [2, 256, 256], replicated
Inputs may be any that keep to these rules, and one draw needn't show every extreme that they name: In every group the counts over the 16 angles sum to 64; some angle of every group has exactly 8.
All inputs are finite; a program needn't handle non-finite values.
Results may differ from a plain program's by a relative error of at most 0.005.
Values may be sent and summed in bfloat16 or wider, within the bound.
A program may use at most 128 MiB of HBM per device.

v0:
```python
import math

import jax
import jax.numpy as jnp
from jax import lax
from jax.sharding import PartitionSpec as P

MEAN_POS = 4


def band_matrix(weights, offsets, extent):
    row_ids = lax.broadcasted_iota(jnp.int32, (extent, extent), 0)
    col_ids = lax.broadcasted_iota(jnp.int32, (extent, extent), 1)
    distance = (col_ids - row_ids)[None]
    summed = jnp.zeros((weights.shape[0], extent, extent), jnp.float32)
    for tap_index in range(weights.shape[1]):
        matches = distance == offsets[:, None, None] + (tap_index - 1)
        summed = summed + jnp.where(
            matches, weights[:, tap_index, None, None].astype(jnp.float32), 0.0
        )
    return summed.astype(jnp.bfloat16)


def dft_tables(extent):
    outer = (
        lax.broadcasted_iota(jnp.int32, (extent, extent), 0)
        * lax.broadcasted_iota(jnp.int32, (extent, extent), 1)
        % extent
    )
    phase = outer.astype(jnp.float32) * (2.0 * math.pi / extent)
    factor = 1.0 / math.sqrt(extent)
    return (jnp.cos(phase) * factor, jnp.sin(phase) * factor)


def left_apply(table, stacked):
    return jnp.einsum("jk,skl->sjl", table, stacked, precision=lax.Precision.HIGHEST)


def right_apply(stacked, table):
    return jnp.einsum("sjk,kl->sjl", stacked, table, precision=lax.Precision.HIGHEST)


def far_field_update(patches, intensity, live_mask, probe_field, norm_factor):
    cosines, sines = dft_tables(patches.shape[-1])
    probe_re = probe_field[0]
    probe_im = probe_field[1]
    patch_re = patches[:, 0]
    patch_im = patches[:, 1]
    wave_re = probe_re * patch_re - probe_im * patch_im
    wave_im = probe_re * patch_im + probe_im * patch_re
    half_re = left_apply(cosines, wave_re) + left_apply(sines, wave_im)
    half_im = left_apply(cosines, wave_im) - left_apply(sines, wave_re)
    far_re = right_apply(half_re, cosines) + right_apply(half_im, sines)
    far_im = right_apply(half_im, cosines) - right_apply(half_re, sines)
    misfit = far_re * far_re + far_im * far_im - intensity
    resid_re = misfit * far_re
    resid_im = misfit * far_im
    inner_re = left_apply(cosines, resid_re) - left_apply(sines, resid_im)
    inner_im = left_apply(cosines, resid_im) + left_apply(sines, resid_re)
    weight_col = (norm_factor * live_mask)[:, None, None]
    chi_re = (right_apply(inner_re, cosines) - right_apply(inner_im, sines)) * weight_col
    chi_im = (right_apply(inner_im, cosines) + right_apply(inner_re, sines)) * weight_col
    patch_grad = jnp.stack(
        [probe_re * chi_re + probe_im * chi_im, probe_re * chi_im - probe_im * chi_re], axis=1
    )
    probe_part = jnp.stack(
        [
            jnp.sum(patch_re * chi_re + patch_im * chi_im, axis=0),
            jnp.sum(patch_re * chi_im - patch_im * chi_re, axis=0),
        ]
    )
    return (patch_grad, probe_part)


def per_device(
    object_field, probe_field, diffraction, scan_offsets, counts, band_weights, band_offsets
):
    angle_id = lax.axis_index("ang")
    ang_count = lax.axis_size("ang")
    slab_count = lax.axis_size("slab")
    extent = object_field.shape[2]
    patch_len = probe_field.shape[-1]
    slot_total = diffraction.shape[2]
    weights_here = lax.dynamic_index_in_dim(band_weights, angle_id, 0, keepdims=False)
    offsets_here = lax.dynamic_index_in_dim(band_offsets, angle_id, 0, keepdims=False)
    matrix_y = band_matrix(weights_here[:, 0], offsets_here[:, 0], extent)
    matrix_x = band_matrix(weights_here[:, 1], offsets_here[:, 1], extent)
    lifted = jnp.einsum(
        "zpy,czyx->czpx", matrix_y, object_field, preferred_element_type=jnp.float32
    ).astype(jnp.bfloat16)
    partial_image = jnp.einsum(
        "czpx,zqx->cpq", lifted, matrix_x, preferred_element_type=jnp.float32
    )
    projection = lax.psum(partial_image, "slab")
    norm_factor = 1.0 / math.sqrt(MEAN_POS * ang_count * slab_count)
    own_count = counts[0, 0]
    corners = scan_offsets[0, 0]
    intensity = diffraction[0, 0]
    patches = jax.vmap(
        lambda corner: lax.dynamic_slice(
            projection, (jnp.int32(0), corner[0], corner[1]), (2, patch_len, patch_len)
        )
    )(corners)
    slot_ids = jnp.arange(slot_total, dtype=jnp.int32)
    live_mask = (slot_ids < own_count).astype(jnp.float32)
    patch_grad, probe_part = far_field_update(
        patches, intensity, live_mask, probe_field, norm_factor
    )
    image = jnp.zeros((2, extent, extent), jnp.float32)
    for slot_id in range(slot_total):
        corner_y = corners[slot_id, 0]
        corner_x = corners[slot_id, 1]
        window = lax.dynamic_slice(
            image, (jnp.int32(0), corner_y, corner_x), (2, patch_len, patch_len)
        )
        image = lax.dynamic_update_slice(
            image, window + patch_grad[slot_id], (jnp.int32(0), corner_y, corner_x)
        )
    image_rows = lax.psum_scatter(image, "slab", scatter_dimension=1, tiled=True)
    probe_grad = lax.psum(probe_part, ("ang", "slab"))
    image_low = lax.all_gather(image_rows.astype(jnp.bfloat16), "slab", axis=1, tiled=True)
    lowered = jnp.einsum(
        "zpy,cpq->yczq", matrix_y, image_low, preferred_element_type=jnp.float32
    ).astype(jnp.bfloat16)
    object_grad = lax.psum_scatter(
        jnp.einsum("yczq,zqx->yczx", lowered, matrix_x, preferred_element_type=jnp.float32),
        "ang",
        scatter_dimension=0,
        tiled=True,
    )
    return (object_grad, probe_grad)


def solution(mesh):
    placed = (
        P(None, "slab", None, None),
        P(),
        P("ang", "slab", None, None, None),
        P("ang", "slab", None, None),
        P("slab", "ang"),
        P(None, "slab", None, None),
        P(None, "slab", None),
    )
    return jax.shard_map(
        per_device,
        mesh=mesh,
        in_specs=placed,
        out_specs=(P("ang", None, "slab", None), P()),
        check_vma=False,
    )
```

profile of v0, /device:TPU:2, one launch (start us, length us, event | category | flops | bytes accessed | tf_op | source)
XLA Modules:
  0.0 1079.7 jit_solution(3519142083504947784)
XLA Ops:
  18.6 17.2 %fusion.2 = f32[2,1024,1024]{2,1,0:T(8,128)} fusion(f32[]{:T(128)S(6)} %convert.11, s32[]{:T(128)} %bitcast.7, f32[]{:T(128)S(6)} %convert.10, s32[]{:T(128)} %bitcast.5, f32[]{:T(128)S(6)} %convert.9, s32[]{:T(128)} %bitcast.3, f32[]{:T(128)S(6)} %convert.8, s32[]{:T(128)} %bitcast, bf16[2,1,1024,1024]{3,2,1,0:T(8,128)(2,1)} %param.7, f32[]{:T(128)S(6)} %convert.15, ...), kind=kOutput, calls=%fused_computation.18 | convolution fusion | flops 8619294720 | bytes 12582976 | tf_op jit(solution)/shard_map/czpx,zqx->cpq/dot_general | solution.py:91
  67.4 311.7 %all-reduce.5.cloned.1.call-done = f32[2,1024,1024]{2,1,0:T(8,128)} async-done(((f32[2,1024,1024]{2,1,0:T(8,128)}), f32[2,1024,1024]{2,1,0:T(8,128)}) %all-reduce.5.cloned.1.call-update) | async-done | bytes 8388624 | tf_op jit(solution)/shard_map/psum | solution.py:94
  379.0 32.8 %while.1 = (s32[]{:T(128)}, f32[2,1024,1024]{2,1,0:T(8,128)}, s32[8,3]{0,1:T(4,128)S(1)}, f32[8,2,256,256]{3,2,0,1:T(8,128)}, s32[]{:T(128)}) while((s32[]{:T(128)}, f32[2,1024,1024]{2,1,0:T(8,128)}, s32[8,3]{0,1:T(4,128)S(1)}, f32[8,2,256,256]{3,2,0,1:T(8,128)}, s32[]{:T(128)}) %tuple.59), condition=%wide.while_cond, body=%wide.while_body.sunk | while | flops 2 | bytes 1050217 | solution.py:100
  379.7 3.5 bitcast_dynamic-update-slice_fusion.2
  383.7 3.4 bitcast_dynamic-update-slice_fusion.2
  387.8 3.5 bitcast_dynamic-update-slice_fusion.2
  391.9 3.5 bitcast_dynamic-update-slice_fusion.2
  396.0 3.4 bitcast_dynamic-update-slice_fusion.2
  400.1 3.5 bitcast_dynamic-update-slice_fusion.2
  404.2 3.4 bitcast_dynamic-update-slice_fusion.2
  408.2 3.4 bitcast_dynamic-update-slice_fusion.2
  411.9 7.0 fusion.119
  418.9 4.6 fusion.116
  423.5 5.0 convolution_subtract_fusion.1
  428.5 4.5 fusion.31
  433.1 4.5 fusion.29
  437.6 4.8 convolution_add_fusion.1
  442.4 4.6 fusion.62
  447.0 4.6 fusion.65
  451.6 4.9 fusion.113
  456.5 4.7 fusion.110
  461.2 5.1 convolution_add_fusion
  466.3 4.5 fusion.21
  470.8 4.5 fusion.23
  475.3 4.9 convolution_subtract_fusion
  480.1 4.7 add_multiply_fusion
  484.9 6.2 fusion.40
  492.4 4.3 broadcast_in_dim.107
  496.7 6.3 dynamic_update_slice.24
  503.0 1.5 fusion.79
  504.5 6.6 dynamic_update_slice.25
  511.0 1.5 fusion.82
  512.5 6.0 dynamic_update_slice.26
  518.5 1.5 fusion.85
  520.0 6.7 dynamic_update_slice.27
  528.2 6.6 dynamic_update_slice.28
  534.7 1.5 fusion.91
  536.2 6.8 dynamic_update_slice.29
  544.4 6.2 dynamic_update_slice.30
  552.0 6.8 dynamic_update_slice.31
  558.9 117.0 %reduce-scatter.2.cloned.1.call-done = f32[2,128,1024]{2,1,0:T(8,128)} async-done(((f32[2,1024,1024]{2,1,0:T(8,128)}), f32[2,128,1024]{2,1,0:T(8,128)}) %reduce-scatter.2.cloned.1.call-update) | async-done | bytes 1048592 | tf_op jit(solution)/shard_map/reduce_scatter | solution.py:119
  675.9 2.1 convert_element_type.95
  678.3 70.1 %all-gather.2.cloned.1.call-done = bf16[2,1024,1024]{2,1,0:T(8,128)(2,1)} async-done(((bf16[2,128,1024]{2,1,0:T(8,128)(2,1)}), bf16[2,1024,1024]{2,1,0:T(8,128)(2,1)}) %all-gather.2.cloned.1.call-update) | async-done | bytes 4194320 | tf_op jit(solution)/shard_map/all_gather | solution.py:121
  748.5 16.5 %fusion.16 = f32[1024,2,1,1024]{0,3,1,2:T(8,128)} fusion(f32[]{:T(128)S(6)} %convert.11, s32[]{:T(128)} %bitcast.7, f32[]{:T(128)S(6)} %convert.10, s32[]{:T(128)} %bitcast.5, f32[]{:T(128)S(6)} %convert.9, s32[]{:T(128)} %bitcast.3, f32[]{:T(128)S(6)} %convert.8, s32[]{:T(128)} %bitcast, bf16[2,1024,1024]{2,1,0:T(8,128)(2,1)} %all-gather.2.cloned.1.call-done, ...), kind=kOutput, calls=%fused_computation.35 | convolution fusion | flops 8619294720 | bytes 12582976 | tf_op jit(solution)/shard_map/yczq,zqx->yczx/dot_general | solution.py:126
  765.0 13.4 %copy.101 = f32[1024,2,1,1024]{3,1,2,0:T(2,128)} copy(f32[1024,2,1,1024]{0,3,1,2:T(8,128)} %fusion.16) | data formatting | bytes 16777216 | tf_op jit(solution)/shard_map/yczq,zqx->yczx/transpose | solution.py:126
  780.5 138.4 %all-reduce.9.cloned.1.call-done = f32[1024,2,1,1024]{3,1,2,0:T(2,128)} async-done(((f32[1024,2,1,1024]{3,1,2,0:T(2,128)}), f32[1024,2,1,1024]{3,1,2,0:T(2,128)}) %all-reduce.9.cloned.1.call-update) | async-done | bytes 8388624
  921.4 149.5 %all-reduce.7.cloned.1.call-done = f32[2,256,256]{2,1,0:T(8,128)} async-done(((f32[2,256,256]{2,1,0:T(8,128)}), f32[2,256,256]{2,1,0:T(8,128)}) %all-reduce.7.cloned.1.call-update) | async-done | bytes 524304 | tf_op jit(solution)/shard_map/psum | solution.py:120
  1070.9 1.9 copy.157
  (62 shorter events, 18.8 us)
Async XLA Ops:
  7.2 5.5 copy-start
  7.2 371.8 %all-reduce.5.cloned.1.call-start = ((), (), s32[]{:S(2)}) async-start(), calls=%async_computation.1 | async-start | bytes 16777216 | tf_op jit(solution)/shard_map/psum | solution.py:94
  35.8 0.7 copy-start.6
  35.8 31.5 %copy-start.5 = (f32[2,256,256]{2,1,0:T(8,128)S(1)}, f32[2,256,256]{2,1,0:T(8,128)}, u32[]{:S(2)}) copy-start(f32[2,256,256]{2,1,0:T(8,128)} %param.8) | copy-start | bytes 1572868
  35.8 640.1 %reduce-scatter.2.cloned.1.call-start = ((), (), s32[]{:S(2)}) async-start(), calls=%async_computation.2 | async-start | bytes 9437184 | tf_op jit(solution)/shard_map/reduce_scatter | solution.py:119
  411.8 7.0 copy-start.4
  447.0 4.6 copy-start.3
  491.1 1.4 copy-start.2
  558.9 189.6 %all-gather.2.cloned.1.call-start = ((), (), s32[]{:S(2)}) async-start(), calls=%async_computation.3 | async-start | bytes 4718592 | tf_op jit(solution)/shard_map/all_gather | solution.py:121
  678.0 240.9 %all-reduce.9.cloned.1.call-start = ((), (), s32[]{:S(2)}) async-start(), calls=%async_computation.5 | async-start | bytes 16777216
  778.3 0.9 copy-start.7
  778.3 292.5 %all-reduce.7.cloned.1.call-start = ((), (), s32[]{:S(2)}) async-start(), calls=%async_computation.4 | async-start | bytes 1048576 | tf_op jit(solution)/shard_map/psum | solution.py:120
  778.4 294.4 %copy-start.1 = (bf16[16,1,2,4]{0,3,2,1:T(4,128)(2,1)S(1)}, bf16[16,1,2,4]{0,3,2,1:T(4,128)(2,1)}, u32[]{:S(2)}) copy-start(bf16[16,1,2,4]{0,3,2,1:T(4,128)(2,1)} %param.12) | copy-start | bytes 772
Sparse Core Ops, SparseCore 0:
  35.9 343.0 all-reduce.4
  559.0 116.8 reduce-scatter.1
  679.1 69.3 all-gather.1
  778.5 140.4 all-reduce.8
  924.9 145.9 all-reduce.6
where the time goes:
time: 1090 us; the launch traced here: 1080 us
  waiting for transfers between devices  787 us (72%)
  matrix products  113 us (10%)
  local copies, waits for them, and re-layouts  112 us (10%)
  between operations  54.3 us (5%)
  other arithmetic  13.2 us (1%)
    psum x1, waiting for transfers between devices, per_device(): projection = lax.psum(partial_image, 'slab')  312 us
    psum x1, waiting for transfers between devices, per_device(): probe_grad = lax.psum(probe_part, ('ang', 'slab'))  150 us
    unnamed x6, waiting for transfers between devices  139 us
    reduce_scatter x1, waiting for transfers between devices, per_device(): lax.psum_scatter(image, 'slab', scatter_dimension=1, tiled=True)  117 us
    all_gather x1, waiting for transfers between devices, per_device(): lax.all_gather(image_rows.astype(jnp.bfloat16), 'slab', axis=1, tiled=True)  70.1 us
    dynamic_update_slice x8, local copies, waits for them, and re-layouts, per_device(): lax.dynamic_update_slice(image, window + patch_grad[slot_id], (jnp.int32(...  51.9 us
    dot_general x8, matrix products, left_apply(): jnp.einsum('jk,skl->sjl', table, stacked, precision=lax.Precision.HIGHEST)  40.9 us
    dot_general x8, matrix products, right_apply(): jnp.einsum('sjk,kl->sjl', stacked, table, precision=lax.Precision.HIGHEST)  38.1 us
  transfers between devices with their start and end apart: 5, of which 5 were waited for; matrix products, arithmetic and copies ran while one was open for 0% of the time, Pallas kernels for 0%

commit v1 on v0

v1 whole, which is shorter than its diff:
```python
import functools
import math

import jax
import jax.numpy as jnp
import numpy as np
from jax import lax
from jax.experimental import pallas as pl
from jax.experimental.pallas import tpu as pltpu
from jax.sharding import PartitionSpec as P

MESH = pl.DeviceIdType.MESH
F32 = jnp.float32
BF16 = jnp.bfloat16
GRID = 1024
PATCH = 256
SLOTS = 8
NSLAB = 8
ROWS = GRID // NSLAB
HALF = ROWS // 2
PAD = 128
HALO = 80
POSITIONS = 512
VMEM_LIMIT = 56 << 20


def block_of(slab):
    return (slab % 2) * 4 + slab // 2


def slab_of(block):
    return (block % 4) * 2 + block // 4


def band(shape, axis_out, start, weights, step):
    inner = lax.broadcasted_iota(jnp.int32, shape, 1 - axis_out)
    outer = lax.broadcasted_iota(jnp.int32, shape, axis_out)
    distance = (inner - outer).astype(F32)
    summed = jnp.zeros(shape, F32)
    for tap, weight in enumerate(weights):
        summed = jnp.where(distance == start + step * tap, weight, summed)
    return summed.astype(BF16)


def encode(values):
    return (values * jnp.abs(values)).astype(BF16)


def decode(codes):
    square = codes.astype(F32)
    return square * lax.rsqrt(jnp.maximum(jnp.abs(square), 1e-37))


def dot(left, right):
    return jnp.dot(left, right, preferred_element_type=F32)


WIDE = GRID // 2
LEFT = pl.ds(0, WIDE)
RIGHT = pl.ds(WIDE, WIDE)


class Post:
    def __init__(self, sends, recvs):
        self.sends = sends
        self.recvs = recvs
        self.opened = []

    def go(self, src, dst, peer):
        k = len(self.opened)
        copy = pltpu.make_async_remote_copy(
            src_ref=src, dst_ref=dst, send_sem=self.sends.at[k], recv_sem=self.recvs.at[k],
            device_id=peer, device_id_type=MESH,
        )
        copy.start()
        self.opened.append(copy)
        return copy

    def finish(self):
        for copy in self.opened:
            copy.wait_send()


class Place:
    def __init__(self):
        self.ang = lax.axis_index("ang")
        self.me = lax.axis_index("slab")
        self.z = self.me // 2
        self.xh = self.me % 2

    def slab(self, dz, other):
        x = 1 - self.xh if other else self.xh
        return lax.rem(self.z + dz, 4) * 2 + x

    def peer(self, dz, other):
        return (self.ang, self.slab(dz, other))

    def block(self, dz, other):
        return block_of(self.slab(dz, other))


class Ring:
    def __init__(self, post, place, bufs, own, first):
        self.post, self.place = post, place
        self.hr, self.fs, self.fr = bufs
        self.own, self.first = own, first

    def start(self):
        self.halves = [
            self.post.go(self.first(k), self.hr.at[k], self.place.peer((1, 3)[k], 0))
            for k in range(2)
        ]

    def middle(self):
        self.whole = []
        for k, dz in enumerate((1, 3)):
            lo = HALF * k
            self.fs[k, HALF - lo : ROWS - lo, :] = encode(self.own(dz, HALF - lo, HALF))
            self.halves[k].wait_recv()
            both = self.own(dz, lo, HALF) + decode(self.hr[k])
            self.fs[k, lo : lo + HALF, :] = encode(both)
            self.whole.append(self.post.go(self.fs.at[k], self.fr.at[k], self.place.peer(dz, 0)))

    def end(self):
        for copy in self.whole:
            copy.wait_recv()
        return self.own(0, 0, ROWS) + decode(self.fr[0]) + decode(self.fr[1])


class Reduce:
    def __init__(self, post, place, part, bufs, own, ref):
        hs, hr, fs, fr, xs, xr = bufs
        self.post, self.place, self.own, self.ref = post, place, own, ref
        self.hs, self.xs, self.xr = hs.at[part], xs.at[part], xr.at[part]
        self.rings = []
        for chain, other in enumerate((1, 0)):
            self.rings.append(
                Ring(
                    post, place, (hr.at[part, chain], fs.at[part, chain], fr.at[part, chain]),
                    functools.partial(self.left, other),
                    functools.partial(self.left_first, other, chain),
                )
            )
        self.rings.append(
            Ring(
                post, place, (hr.at[part, 2], fs.at[part, 2], fr.at[part, 2]),
                self.right, self.right_first,
            )
        )
        self.crossing = {}

    def left(self, other, dz, lo, n):
        return self.own(dz, other, lo, n, LEFT)

    def left_first(self, other, chain, k):
        return self.ref(2, other, HALF * k, HALF, LEFT, self.hs.at[chain, k])

    def right(self, dz, lo, n):
        return self.own(dz, 0, lo, n, RIGHT) + decode(self.xr[dz, lo : lo + n, :])

    def right_first(self, k):
        self.hs[2, k] = encode(self.right(2, HALF * k, HALF))
        return self.hs.at[2, k]

    def start_far(self, other):
        self.rings[1 - other].start()

    def start_cross(self, dz):
        src = self.ref(dz, 1, 0, ROWS, RIGHT, self.xs.at[dz])
        self.crossing[dz] = self.post.go(src, self.xr.at[dz], self.place.peer(0, 1))

    def stage1(self):
        self.rings[0].middle()
        self.rings[1].middle()

    def stage2(self):
        self.crossing[2].wait_recv()
        self.rings[2].start()

    def stage3(self):
        self.xs[4] = encode(self.rings[0].end())
        self.crossing[4] = self.post.go(self.xs.at[4], self.xr.at[4], self.place.peer(0, 1))

    def stage4(self):
        self.crossing[1].wait_recv()
        self.crossing[3].wait_recv()
        self.rings[2].middle()

    def stage5(self):
        mine = self.rings[1].end()
        self.crossing[4].wait_recv()
        return mine + decode(self.xr[4])

    def stage6(self):
        self.crossing[0].wait_recv()
        return self.rings[2].end()


def reduce_scratch():
    code = BF16
    return [
        pltpu.VMEM((2, 3, 2, HALF, WIDE), code),
        pltpu.VMEM((2, 3, 2, HALF, WIDE), code),
        pltpu.VMEM((2, 3, 2, ROWS, WIDE), code),
        pltpu.VMEM((2, 3, 2, ROWS, WIDE), code),
        pltpu.VMEM((2, 5, ROWS, WIDE), code),
        pltpu.VMEM((2, 5, ROWS, WIDE), code),
    ]


class Gather:
    def __init__(self, post, place, part, whole):
        self.post, self.place, self.part, self.whole = post, place, part, whole

    def span(self, dz, other, cols, lo=0, n=ROWS):
        start = pl.multiple_of(self.place.block(dz, other) * ROWS + lo, HALF)
        return self.whole.at[self.part, pl.ds(start, n), cols]

    def send(self, dz, other, cols, to_dz, to_other, lo=0, n=ROWS):
        span = self.span(dz, other, cols, lo, n)
        return self.post.go(span, span, self.place.peer(to_dz, to_other))

    def spread(self, other, cols):
        return [self.send(0, other, cols, dz, 0) for dz in (1, 3)]

    def relay(self, other, cols, pair):
        pair[0].wait_recv()
        first = self.send(3, other, cols, 1, 0, 0, HALF)
        pair[1].wait_recv()
        return [first, self.send(1, other, cols, 3, 0, HALF, HALF)]

    def stage0(self):
        self.cross_left = self.send(0, 0, LEFT, 0, 1)
        self.right = self.spread(0, RIGHT)
        self.cross_right = [self.send(0, 0, RIGHT, 0, 1)]
        self.left = self.spread(0, LEFT)

    def stage1(self):
        self.right_far = self.relay(0, RIGHT, self.right)
        for dz in (3, 1):
            self.cross_right.append(self.send(dz, 0, RIGHT, 0, 1))

    def stage2(self):
        self.cross_left.wait_recv()
        self.left_other = self.spread(1, LEFT)

    def stage3(self):
        self.left_far = self.relay(0, LEFT, self.left)

    def stage4(self):
        for copy in self.right_far:
            copy.wait_recv()
        self.cross_right.append(self.send(2, 0, RIGHT, 0, 1))

    def stage5(self):
        self.left_far += self.relay(1, LEFT, self.left_other)

    def stage6(self):
        for copy in self.left_far + self.cross_right:
            copy.wait_recv()


def greet(place):
    barrier = pltpu.get_barrier_semaphore()
    for dz in range(4):
        for other in range(2):
            if (dz, other) != (0, 0):
                pl.semaphore_signal(
                    barrier, inc=1, device_id=place.peer(dz, other), device_id_type=MESH
                )
    return barrier


def run_reduces(first, second, done):
    first.stage1()
    second.stage1()
    first.stage2()
    first.stage3()
    second.stage2()
    first.stage4()
    second.stage3()
    left = first.stage5()
    right = first.stage6()
    done(0, left, right)
    second.stage4()
    left = second.stage5()
    right = second.stage6()
    done(1, left, right)


def forward_kernel(
    offs, wts, par, obj, proj, par_all,
    opad, lift, t0, t1, dbuf, hs, hr, fs, fr, xs, xr,
    load_sem, sends, recvs,
):
    place = Place()
    barrier = greet(place)
    load = pltpu.make_async_copy(obj, opad.at[:, pl.ds(PAD, GRID), :], load_sem)
    load.start()
    opad[:, :PAD, :] = jnp.zeros((2, PAD, GRID), BF16)
    opad[:, PAD + GRID :, :] = jnp.zeros((2, PAD, GRID), BF16)
    lift[:, :PAD] = jnp.zeros((2 * ROWS, PAD), BF16)
    lift[:, PAD + GRID :] = jnp.zeros((2 * ROWS, PAD), BF16)
    off_y = offs[0]
    off_x = offs[1]
    t0[...] = band(t0.shape, 0, (off_y + PAD - 1).astype(F32), [wts[t] for t in range(4)], 1)
    t1[...] = band(t1.shape, 1, (off_x + PAD - 1).astype(F32), [wts[4 + t] for t in range(4)], 1)
    load.wait()

    par_all[pl.ds(place.me, 1)] = par[...][None]
    pl.semaphore_wait(barrier, NSLAB - 1)
    post = Post(sends, recvs)
    par_copies = []
    for dz in range(4):
        for other in range(2):
            if (dz, other) != (0, 0):
                span = par_all.at[place.me]
                par_copies.append(post.go(span, span, place.peer(dz, other)))

    def slot(dz, other):
        return 2 * dz + other

    def project(dz, other):
        start = pl.multiple_of(place.block(dz, other) * ROWS, ROWS)
        for part in range(2):
            rows = opad[part, pl.ds(start, 3 * PAD), :]
            lift[part * ROWS : (part + 1) * ROWS, PAD : PAD + GRID] = dot(t0[...], rows).astype(BF16)
        for q in range(GRID // 256):
            tile = dot(lift[:, 256 * q : 256 * q + 512], t1[...])
            dbuf[slot(dz, other), :, :, 256 * q : 256 * q + 256] = tile.reshape(2, ROWS, 256)

    bufs = (hs, hr, fs, fr, xs, xr)
    reduces = []
    for part in range(2):

        def own(dz, other, lo, n, cols, part=part):
            return dbuf[slot(dz, other), part, pl.ds(lo, n), cols]

        def ref(dz, other, lo, n, cols, room, part=part):
            room[...] = encode(own(dz, other, lo, n, cols, part))
            return room

        reduces.append(Reduce(post, place, part, bufs, own, ref))
    for dz, other in ((2, 1), (2, 0), (1, 1), (3, 1), (0, 1), (1, 0), (3, 0), (0, 0)):
        project(dz, other)
        for reduce in reduces:
            if dz == 2:
                reduce.start_far(other)
            if other == 1:
                reduce.start_cross(dz)
    rows = pl.ds(pl.multiple_of(place.block(0, 0) * ROWS, ROWS), ROWS)
    gathers = [Gather(post, place, part, proj) for part in range(2)]

    def done(part, left, right):
        proj[part, rows, LEFT] = encode(left)
        proj[part, rows, RIGHT] = encode(right)
        gathers[part].stage0()

    run_reduces(reduces[0], reduces[1], done)
    for k in range(1, 7):
        for gather in gathers:
            getattr(gather, "stage%d" % k)()
    for copy in par_copies:
        copy.wait_recv()
    post.finish()


def forward(offs, wts, par, obj):
    return pl.pallas_call(
        forward_kernel,
        out_shape=(
            jax.ShapeDtypeStruct((2, GRID, GRID), BF16),
            jax.ShapeDtypeStruct((NSLAB, 16, 512), F32),
        ),
        in_specs=[
            pl.BlockSpec(memory_space=pltpu.SMEM),
            pl.BlockSpec(memory_space=pltpu.SMEM),
            pl.BlockSpec(memory_space=pltpu.VMEM),
            pl.BlockSpec(memory_space=pl.ANY),
        ],
        out_specs=(
            pl.BlockSpec(memory_space=pltpu.VMEM),
            pl.BlockSpec(memory_space=pltpu.VMEM),
        ),
        scratch_shapes=[
            pltpu.VMEM((2, GRID + 2 * PAD, GRID), BF16),
            pltpu.VMEM((2 * ROWS, GRID + 2 * PAD), BF16),
            pltpu.VMEM((ROWS, 3 * PAD), BF16),
            pltpu.VMEM((512, 256), BF16),
            pltpu.VMEM((NSLAB, 2, ROWS, GRID), F32),
        ]
        + reduce_scratch()
        + [
            pltpu.SemaphoreType.DMA,
            pltpu.SemaphoreType.DMA((96,)),
            pltpu.SemaphoreType.DMA((96,)),
        ],
        compiler_params=pltpu.CompilerParams(
            collective_id=0, has_side_effects=True, vmem_limit_bytes=VMEM_LIMIT
        ),
        name="forward",
    )(offs, wts, par, obj)


def dft_tables():
    index = np.arange(PATCH)
    phase = 2.0 * np.pi * ((index[:, None] * index[None, :]) % PATCH) / PATCH
    cosines = np.cos(phase) / math.sqrt(PATCH)
    sines = np.sin(phase) / math.sqrt(PATCH)
    whole = np.block([[cosines, -sines], [sines, cosines]]).astype(np.float32)
    high = whole.astype(jnp.bfloat16)
    low = (whole - high.astype(np.float32)).astype(jnp.bfloat16)
    across = np.concatenate([high, high, low], axis=1)
    across_t = np.concatenate([high.T, high.T, low.T], axis=1)
    return across_t, np.ascontiguousarray(across_t.T), across, np.ascontiguousarray(across.T)


def split_join(values, axis):
    high = values.astype(BF16)
    low = (values - high.astype(F32)).astype(BF16)
    return jnp.concatenate([high, low, high], axis=axis)


def slots_kernel(
    corners, count, proj, probe, diff, left_f, right_f, left_i, right_i,
    image, probe_part, wide, total,
):
    slot = pl.program_id(0)

    @pl.when(slot == 0)
    def _():
        for tile in range(GRID // 128):
            wide[:, tile] = decode(proj[:, :, 128 * tile : 128 * tile + 128])
        total[...] = jnp.zeros(total.shape, F32)
        probe_part[...] = jnp.zeros(probe_part.shape, F32)

    @pl.when(slot < count[0])
    def _():
        row = corners[slot, 0]
        col = corners[slot, 1]
        turn = lax.rem(col, 128)
        tile = col // 128
        lane = lax.broadcasted_iota(jnp.int32, (PATCH, 128), 1)
        early = lane < turn
        patch = []
        for part in range(2):
            window = [wide[part, tile + k, pl.ds(row, PATCH), :] for k in range(3)]
            joined = jnp.concatenate([jnp.where(early, window[2], window[0]), window[1]], axis=1)
            patch.append(pltpu.roll(joined, lax.rem(PATCH - turn, PATCH), 1))
        patch_re, patch_im = patch
        probe_re = probe[0]
        probe_im = probe[1]
        wave = jnp.concatenate(
            [
                probe_re * patch_re - probe_im * patch_im,
                probe_re * patch_im + probe_im * patch_re,
            ],
            axis=0,
        )
        half = dot(left_f[...], split_join(wave, 0))
        half = jnp.concatenate([half[:PATCH], half[PATCH:]], axis=1)
        far = dot(split_join(half, 1), right_f[...])
        far_re = far[:, :PATCH]
        far_im = far[:, PATCH:]
        misfit = (far_re * far_re + far_im * far_im - diff[0]) * (1.0 / math.sqrt(POSITIONS))
        resid = jnp.concatenate([misfit * far_re, misfit * far_im], axis=0)
        inner = dot(left_i[...], split_join(resid, 0))
        inner = jnp.concatenate([inner[:PATCH], inner[PATCH:]], axis=1)
        chi = dot(split_join(inner, 1), right_i[...])
        chi_re = chi[:, :PATCH]
        chi_im = chi[:, PATCH:]
        probe_part[0] += patch_re * chi_re + patch_im * chi_im
        probe_part[1] += patch_re * chi_im - patch_im * chi_re
        grads = (
            probe_re * chi_re + probe_im * chi_im,
            probe_re * chi_im - probe_im * chi_re,
        )
        zero = jnp.zeros((PATCH, 128), F32)
        for part in range(2):
            turned = pltpu.roll(grads[part], turn, 1)
            head = turned[:, :128]
            spread = (jnp.where(early, zero, head), turned[:, 128:], jnp.where(early, head, zero))
            for k in range(3):
                total[part, tile + k, pl.ds(row, PATCH), :] += spread[k]

    @pl.when(slot == SLOTS - 1)
    def _():
        for tile in range(GRID // 128):
            image[:, :, 128 * tile : 128 * tile + 128] = encode(total[:, tile])


def slots(corners, count, proj, probe, diffraction):
    tables = [jnp.asarray(t) for t in dft_tables()]
    whole = pl.BlockSpec(memory_space=pltpu.VMEM)
    scalar = pl.BlockSpec(memory_space=pltpu.SMEM)
    return pl.pallas_call(
        slots_kernel,
        grid=(SLOTS,),
        out_shape=(
            jax.ShapeDtypeStruct((2, GRID, GRID), BF16),
            jax.ShapeDtypeStruct((2, PATCH, PATCH), F32),
        ),
        in_specs=[
            scalar, scalar, whole, whole,
            pl.BlockSpec((1, PATCH, PATCH), lambda i: (i, 0, 0)),
            whole, whole, whole, whole,
        ],
        out_specs=(whole, whole),
        scratch_shapes=[
            pltpu.VMEM((2, GRID // 128 + 1, GRID, 128), F32),
            pltpu.VMEM((2, GRID // 128 + 1, GRID, 128), F32),
        ],
        compiler_params=pltpu.CompilerParams(vmem_limit_bytes=VMEM_LIMIT),
        name="slots",
    )(corners, count, proj, probe, diffraction, *tables)


def backward_kernel(
    image, par_all, probe_part, result, probe_out,
    t0, t1, ext, padded, gbuf, cbuf, hbuf, bbuf, fin,
    pbuf, pacc, pcore, py, pxl, psum, hs, hr, fs, fr, xs, xr,
    sends, recvs, fsend, frecv,
):
    place = Place()
    ang, me, z, xh = place.ang, place.me, place.z, place.xh
    core = lax.rem(ang, 2)
    chip = ang // 2
    y = lax.rem(chip, 4)
    xl = chip // 4
    mine = place.block(0, 0)

    def ang_id(xl_, y_, core_):
        return (xl_ * 4 + y_) * 2 + core_

    def chip_peer(j):
        return (lax.rem(chip + j, 8) * 2 + core, me)

    core_peer = (ang_id(xl, y, 1 - core), me)
    turn_peer = (ang_id(xh, z, core), y * 2 + xl)
    stays = jnp.logical_and(xl == xh, y == z)
    above = (ang, slab_of(lax.rem(mine + NSLAB - 1, NSLAB)))
    below = (ang, slab_of(lax.rem(mine + 1, NSLAB)))

    barrier = greet(place)
    for j in range(1, NSLAB):
        pl.semaphore_signal(barrier, inc=1, device_id=chip_peer(j), device_id_type=MESH)
    pl.semaphore_signal(barrier, inc=1, device_id=core_peer, device_id_type=MESH)

    @pl.when(jnp.logical_not(stays))
    def _():
        pl.semaphore_signal(barrier, inc=1, device_id=turn_peer, device_id_type=MESH)

    def tables(s, carry):
        rows = [par_all[s, k : k + 1, :] for k in range(10)]
        t0[pl.ds(pl.multiple_of(s * ROWS, ROWS), ROWS), :] = band(
            (ROWS, 384), 0, HALO + 1 - rows[8][:, :384], [r[:, :384] for r in rows[:4]], -1
        )
        t1[s] = band((512, 256), 1, PAD + 1 - rows[9][:, :256], [r[:, :256] for r in rows[4:8]], -1)
        return carry

    lax.fori_loop(0, NSLAB, tables, 0)
    ext[:, HALO + ROWS + HALO :, :] = jnp.zeros((2, 384 - ROWS - 2 * HALO, GRID), BF16)
    padded[:, :PAD] = jnp.zeros((NSLAB * ROWS, PAD), BF16)
    padded[:, PAD + GRID :] = jnp.zeros((NSLAB * ROWS, PAD), BF16)
    pl.semaphore_wait(barrier, 2 * (NSLAB - 1) + 1 + jnp.where(stays, 0, 1))

    post = Post(sends, recvs)
    peers = [(dz, other) for dz in range(4) for other in range(2)][1:]
    bufs = (hs, hr, fs, fr, xs, xr)
    reduces = []
    for part in range(2):

        def ref(dz, other, lo, n, cols, room, part=part):
            start = pl.multiple_of(place.block(dz, other) * ROWS + lo, HALF)
            return image.at[part, pl.ds(start, n), cols]

        def own(dz, other, lo, n, cols, part=part, ref=ref):
            return decode(ref(dz, other, lo, n, cols, None)[...])

        reduces.append(Reduce(post, place, part, bufs, own, ref))
    first, second = reduces

    def open_reduce(reduce):
        for dz in (2, 1, 3, 0):
            reduce.start_cross(dz)
            if dz == 2:
                reduce.start_far(1)
                reduce.start_far(0)

    halos = {}

    def finish_reduce(part, reduce):
        ext[part, HALO : HALO + ROWS, LEFT] = reduce.stage5().astype(BF16)
        ext[part, HALO : HALO + ROWS, RIGHT] = reduce.stage6().astype(BF16)
        halos[part] = [
            post.go(ext.at[part, pl.ds(HALO, HALO), :], ext.at[part, pl.ds(HALO + ROWS, HALO), :], above),
            post.go(ext.at[part, pl.ds(ROWS, HALO), :], ext.at[part, pl.ds(0, HALO), :], below),
        ]

    cores = {}

    def spread_slices(part):
        for copy in halos[part]:
            copy.wait_recv()

        @pl.when(mine == 0)
        def _():
            ext[part, :HALO, :] = jnp.zeros((HALO, GRID), BF16)

        @pl.when(mine == NSLAB - 1)
        def _():
            ext[part, HALO + ROWS : 2 * HALO + ROWS, :] = jnp.zeros((HALO, GRID), BF16)

        for q in range(GRID // 256):
            cols = pl.ds(256 * q, 256)
            padded[:, PAD + 256 * q : PAD + 256 * q + 256] = dot(t0[...], ext[part, :, cols]).astype(BF16)

        def slice_step(s, carry):
            rows = pl.ds(pl.multiple_of(s * ROWS, ROWS), ROWS)
            stack = jnp.concatenate(
                [padded[rows, 256 * q : 256 * q + 512] for q in range(GRID // 256)], axis=0
            )
            tiles = encode(dot(stack, t1[s]))
            for q in range(GRID // 256):
                cols = slice(256 * q, 256 * q + 256)
                for half in range(2):
                    lo = ROWS * q + HALF * half
                    gbuf[part, half, s, :, cols] = tiles[lo : lo + HALF]
            return carry

        cores[part] = []
        for k in range(2):
            lax.fori_loop(4 * k, 4 * k + 4, slice_step, 0)
            group = pl.ds(4 * k, 4)
            cores[part].append(
                post.go(gbuf.at[part, 1 - core, group], cbuf.at[part, group], core_peer)
            )

    chips = {}

    def combine(part):
        for copy in cores[part]:
            copy.wait_recv()
        chips[part] = []
        for j in (4, 6, 2, 5, 7, 1, 3, 0):
            target = lax.rem(chip + j, 8)
            s = lax.rem(target, 4) * 2 + target // 4
            both = decode(gbuf[part, core, s]) + decode(cbuf[part, s])
            hbuf[part, j] = encode(both)
            if j:
                chips[part].append(post.go(hbuf.at[part, j], bbuf.at[part, j], chip_peer(j)))

    def turn_copy(part):
        return pltpu.make_async_remote_copy(
            src_ref=fin.at[part], dst_ref=result.at[part], send_sem=fsend.at[part],
            recv_sem=frecv.at[part], device_id=turn_peer, device_id_type=MESH,
        )

    def settle(part):
        for copy in chips[part]:
            copy.wait_recv()
        total = decode(hbuf[part, 0])
        for j in range(1, NSLAB):
            total = total + decode(bbuf[part, j])
        fin[part] = encode(total)

        @pl.when(stays)
        def _():
            result[part] = fin[part]

        @pl.when(jnp.logical_not(stays))
        def _():
            turn_copy(part).start()

    open_reduce(first)
    probe_copies = []
    for dz, other in peers:
        dest = place.slab(dz, other)
        rows = pl.ds(pl.multiple_of(dest * 64, 64), 64)
        probe_copies.append(
            post.go(probe_part.at[rows, :], pbuf.at[2 * dz + other], place.peer(dz, other))
        )
    first.stage1()
    open_reduce(second)
    first.stage2()
    first.stage3()
    first.stage4()
    second.stage1()
    second.stage2()
    finish_reduce(0, first)
    second.stage3()

    total = probe_part[pl.ds(pl.multiple_of(me * 64, 64), 64), :]
    for copy, (dz, other) in zip(probe_copies, peers):
        copy.wait_recv()
        total = total + pbuf[2 * dz + other]
    pacc[...] = total
    core_probe = post.go(pacc, pcore, core_peer)

    second.stage4()
    spread_slices(0)
    finish_reduce(1, second)

    core_probe.wait_recv()
    psum[0] = pacc[...] + pcore[...]
    y_copies = [
        post.go(psum.at[0], py.at[j], (ang_id(xl, lax.rem(y + j, 4), core), me)) for j in range(1, 4)
    ]
    combine(0)
    spread_slices(1)
    for copy in y_copies:
        copy.wait_recv()
    psum[1] = (psum[0] + py[1]) + (py[2] + py[3])
    xl_probe = post.go(psum.at[1], pxl, (ang_id(1 - xl, y, core), me))
    combine(1)
    settle(0)
    xl_probe.wait_recv()
    span = probe_out.at[pl.ds(pl.multiple_of(me * 64, 64), 64), :]
    span[...] = psum[1] + pxl[...]
    out_copies = [post.go(span, span, place.peer(*peer)) for peer in peers]
    settle(1)
    for copy in out_copies:
        copy.wait_recv()

    @pl.when(jnp.logical_not(stays))
    def _():
        turn_copy(0).wait()
        turn_copy(1).wait()

    post.finish()


def backward(image, par_all, probe_part):
    whole = pl.BlockSpec(memory_space=pltpu.VMEM)
    dma = pltpu.SemaphoreType.DMA
    return pl.pallas_call(
        backward_kernel,
        out_shape=(
            jax.ShapeDtypeStruct((2, HALF, GRID), BF16),
            jax.ShapeDtypeStruct((2 * PATCH, PATCH), F32),
        ),
        in_specs=[whole] * 3,
        out_specs=(whole, whole),
        scratch_shapes=[
            pltpu.VMEM((NSLAB * ROWS, 384), BF16),
            pltpu.VMEM((NSLAB, 512, 256), BF16),
            pltpu.VMEM((2, 384, GRID), BF16),
            pltpu.VMEM((NSLAB * ROWS, GRID + 2 * PAD), BF16),
            pltpu.VMEM((2, 2, NSLAB, HALF, GRID), BF16),
            pltpu.VMEM((2, NSLAB, HALF, GRID), BF16),
            pltpu.VMEM((2, NSLAB, HALF, GRID), BF16),
            pltpu.VMEM((2, NSLAB, HALF, GRID), BF16),
            pltpu.VMEM((2, HALF, GRID), BF16),
            pltpu.VMEM((NSLAB, 64, PATCH), F32),
            pltpu.VMEM((64, PATCH), F32),
            pltpu.VMEM((64, PATCH), F32),
            pltpu.VMEM((4, 64, PATCH), F32),
            pltpu.VMEM((64, PATCH), F32),
            pltpu.VMEM((2, 64, PATCH), F32),
        ]
        + reduce_scratch()
        + [dma((96,)), dma((96,)), dma((2,)), dma((2,))],
        compiler_params=pltpu.CompilerParams(
            collective_id=1, has_side_effects=True, vmem_limit_bytes=VMEM_LIMIT
        ),
        name="backward",
    )(image, par_all, probe_part)


def per_device(
    object_field, probe_field, diffraction, scan_offsets, counts, band_weights, band_offsets
):
    ang = lax.axis_index("ang")
    weights = lax.dynamic_index_in_dim(band_weights, ang, 0, keepdims=False)[0]
    offsets = lax.dynamic_index_in_dim(band_offsets, ang, 0, keepdims=False)[0]
    weights = weights.astype(F32).reshape(8)
    par = jnp.concatenate([weights, offsets.astype(F32), jnp.zeros((6,), F32)])
    par = jnp.broadcast_to(par[:, None], (16, 512))
    proj, par_all = forward(offsets, weights, par, object_field.reshape(2, GRID, GRID))
    image, probe_part = slots(
        scan_offsets[0, 0], counts[0], proj, probe_field, diffraction[0, 0]
    )
    result, probe_out = backward(image, par_all, probe_part.reshape(2 * PATCH, PATCH))
    object_grad = decode(jnp.transpose(result, (1, 0, 2)))[:, :, None, :]
    return (object_grad, probe_out.reshape(2, PATCH, PATCH))


def solution(mesh):
    placed = (
        P(None, "slab", None, None),
        P(),
        P("ang", "slab", None, None, None),
        P("ang", "slab", None, None),
        P("slab", "ang"),
        P(None, "slab", None, None),
        P(None, "slab", None),
    )
    return jax.shard_map(
        per_device,
        mesh=mesh,
        in_specs=placed,
        out_specs=(P("ang", None, "slab", None), P()),
        check_vma=False,
    )
```

time: 1090 us -> 217 us (0.20)
  the two profiles are of different devices: /device:TPU:2 before, /device:TPU:66 now
where the time goes in v1:
time: 217 us
  Pallas kernels  209 us (96%)
  local copies, waits for them, and re-layouts  4.46 us (2%)
    pallas_call x1, Pallas kernels, backward(): pl.pallas_call(backward_kernel, out_shape=(jax.ShapeDtypeStruct((2, HALF,...  117 us
    pallas_call x1, Pallas kernels, forward(): pl.pallas_call(forward_kernel, out_shape=(jax.ShapeDtypeStruct((2, GRID,...  71 us
    pallas_call x1, Pallas kernels, slots(): pl.pallas_call(slots_kernel, grid=(SLOTS,), out_shape=(jax.ShapeDtypeStru...  20.8 us

profile of v1, /device:TPU:66, one launch (start us, length us, event | category | flops | bytes accessed | tf_op | source)
XLA Modules:
  0.0 217.0 jit_solution(6997376276300205072)
XLA Ops:
  0.6 0.0 copy-start
  1.3 0.0 copy-done
  1.3 0.2 dynamic-slice_reduce_fusion.offs
  1.5 0.0 copy-start.2
  1.5 0.8 convert_reduce_fusion
  2.4 0.1 reshape.23.wts
  2.4 0.0 copy-start.3
  2.4 0.1 pad_maximum_fusion
  2.5 1.3 copy.15.corners
  3.9 0.7 broadcast_in_dim.4.par
  4.6 0.0 copy-done.2
  4.6 0.0 copy-done.3
  4.6 71.0 %forward.1 = (bf16[2,1024,1024]{2,1,0:T(8,128)(2,1)}, f32[8,16,512]{2,1,0:T(8,128)}) custom-call(s32[2]{0:T(128)} %copy-done.2, f32[8]{0:T(128)} %copy-done.3, f32[16,512]{1,0:T(8,128)} %broadcast_in_dim.4.par, bf16[2,1024,1024]{2,1,0:T(8,128)(2,1)} %bitcast.20), custom_call_target="tpu_custom_call" | custom-call | tf_op jit(solution)/shard_map/forward/pallas_call | solution.py:369
  75.6 20.8 %slots.1 = (bf16[2,1024,1024]{2,1,0:T(8,128)(2,1)}, f32[2,256,256]{2,1,0:T(8,128)}) custom-call(s32[8,2]{1,0:T(8,128)} %copy.15.corners, s32[1]{0:T(128)} %bitcast.19.count, bf16[2,1024,1024]{2,1,0:T(8,128)(2,1)} %get-tuple-element.8.proj, f32[2,256,256]{2,1,0:T(8,128)} %probe.1, f32[8,256,256]{2,1,0:T(8,128)} %bitcast.21, ...), custom_call_target="tpu_custom_call" | custom-call | tf_op jit(solution)/shard_map/slots/pallas_call | solution.py:496
  96.4 117.3 %backward.1 = (bf16[2,64,1024]{2,1,0:T(8,128)(2,1)}, f32[512,256]{1,0:T(8,128)}) custom-call(bf16[2,1024,1024]{2,1,0:T(8,128)(2,1)} %get-tuple-element.9.image, f32[8,16,512]{2,1,0:T(8,128)} %get-tuple-element.10.par_all, f32[512,256]{1,0:T(8,128)} %bitcast.22), custom_call_target="tpu_custom_call" | custom-call | tf_op jit(solution)/shard_map/backward/pallas_call | solution.py:736
  213.7 0.0 copy-start.1
  213.7 1.1 fusion.2
  214.8 1.3 copy.16
  216.2 0.0 copy-done.1
  216.2 0.8 copy.19
  (2 shorter events, 0.0 us)
Async XLA Ops:
  0.6 0.7 copy-start
  1.5 3.1 %copy-start.2 = (s32[2]{0:T(128)}, s32[2]{0:T(128)S(1)}, u32[]{:S(2)}) copy-start(s32[2]{0:T(128)S(1)} %dynamic-slice_reduce_fusion.offs) | copy-start | bytes 28
  2.4 2.1 copy-start.3
  213.7 2.5 %copy-start.1 = (f32[512,256]{1,0:T(8,128)S(1)}, f32[512,256]{1,0:T(8,128)}, u32[]{:S(2)}) copy-start(f32[512,256]{1,0:T(8,128)} %get-tuple-element.13) | copy-start | bytes 1572868

commit v2 on v1

--- a/solution.py
+++ b/solution.py
@@ -51,6 +51,17 @@
     return square * lax.rsqrt(jnp.maximum(jnp.abs(square), 1e-37))
 
 
+def encode_fine(values):
+    square = values * jnp.abs(values) * 2.0**32
+    return (square * jnp.abs(square)).astype(BF16)
+
+
+def decode_fine(codes):
+    fourth = codes.astype(F32)
+    square = fourth * lax.rsqrt(jnp.maximum(jnp.abs(fourth), 1e-37))
+    return square * (lax.rsqrt(jnp.maximum(jnp.abs(square), 1e-30)) * 2.0**-16)
+
+
 def dot(left, right):
     return jnp.dot(left, right, preferred_element_type=F32)
 
@@ -100,8 +111,9 @@
 
 
 class Ring:
-    def __init__(self, post, place, bufs, own, first):
+    def __init__(self, post, place, bufs, own, first, codec):
         self.post, self.place = post, place
+        self.encode, self.decode = codec
         self.hr, self.fs, self.fr = bufs
         self.own, self.first = own, first
 
@@ -115,22 +127,23 @@
         self.whole = []
         for k, dz in enumerate((1, 3)):
             lo = HALF * k
-            self.fs[k, HALF - lo : ROWS - lo, :] = encode(self.own(dz, HALF - lo, HALF))
+            self.fs[k, HALF - lo : ROWS - lo, :] = self.encode(self.own(dz, HALF - lo, HALF))
             self.halves[k].wait_recv()
-            both = self.own(dz, lo, HALF) + decode(self.hr[k])
-            self.fs[k, lo : lo + HALF, :] = encode(both)
+            both = self.own(dz, lo, HALF) + self.decode(self.hr[k])
+            self.fs[k, lo : lo + HALF, :] = self.encode(both)
             self.whole.append(self.post.go(self.fs.at[k], self.fr.at[k], self.place.peer(dz, 0)))
 
     def end(self):
         for copy in self.whole:
             copy.wait_recv()
-        return self.own(0, 0, ROWS) + decode(self.fr[0]) + decode(self.fr[1])
+        return self.own(0, 0, ROWS) + self.decode(self.fr[0]) + self.decode(self.fr[1])
 
 
 class Reduce:
-    def __init__(self, post, place, part, bufs, own, ref):
+    def __init__(self, post, place, part, bufs, own, ref, codec):
         hs, hr, fs, fr, xs, xr = bufs
         self.post, self.place, self.own, self.ref = post, place, own, ref
+        self.encode, self.decode = codec
         self.hs, self.xs, self.xr = hs.at[part], xs.at[part], xr.at[part]
         self.rings = []
         for chain, other in enumerate((1, 0)):
@@ -138,13 +151,13 @@
                 Ring(
                     post, place, (hr.at[part, chain], fs.at[part, chain], fr.at[part, chain]),
                     functools.partial(self.left, other),
-                    functools.partial(self.left_first, other, chain),
+                    functools.partial(self.left_first, other, chain), codec,
                 )
             )
         self.rings.append(
             Ring(
                 post, place, (hr.at[part, 2], fs.at[part, 2], fr.at[part, 2]),
-                self.right, self.right_first,
+                self.right, self.right_first, codec,
             )
         )
         self.crossing = {}
@@ -156,10 +169,10 @@
         return self.ref(2, other, HALF * k, HALF, LEFT, self.hs.at[chain, k])
 
     def right(self, dz, lo, n):
-        return self.own(dz, 0, lo, n, RIGHT) + decode(self.xr[dz, lo : lo + n, :])
+        return self.own(dz, 0, lo, n, RIGHT) + self.decode(self.xr[dz, lo : lo + n, :])
 
     def right_first(self, k):
-        self.hs[2, k] = encode(self.right(2, HALF * k, HALF))
+        self.hs[2, k] = self.encode(self.right(2, HALF * k, HALF))
         return self.hs.at[2, k]
 
     def start_far(self, other):
@@ -178,7 +191,7 @@
         self.rings[2].start()
 
     def stage3(self):
-        self.xs[4] = encode(self.rings[0].end())
+        self.xs[4] = self.encode(self.rings[0].end())
         self.crossing[4] = self.post.go(self.xs.at[4], self.xr.at[4], self.place.peer(0, 1))
 
     def stage4(self):
@@ -189,7 +202,7 @@
     def stage5(self):
         mine = self.rings[1].end()
         self.crossing[4].wait_recv()
-        return mine + decode(self.xr[4])
+        return mine + self.decode(self.xr[4])
 
     def stage6(self):
         self.crossing[0].wait_recv()
@@ -337,10 +350,10 @@
             return dbuf[slot(dz, other), part, pl.ds(lo, n), cols]
 
         def ref(dz, other, lo, n, cols, room, part=part):
-            room[...] = encode(own(dz, other, lo, n, cols, part))
+            room[...] = encode_fine(own(dz, other, lo, n, cols, part))
             return room
 
-        reduces.append(Reduce(post, place, part, bufs, own, ref))
+        reduces.append(Reduce(post, place, part, bufs, own, ref, (encode_fine, decode_fine)))
     for dz, other in ((2, 1), (2, 0), (1, 1), (3, 1), (0, 1), (1, 0), (3, 0), (0, 0)):
         project(dz, other)
         for reduce in reduces:
@@ -352,8 +365,8 @@
     gathers = [Gather(post, place, part, proj) for part in range(2)]
 
     def done(part, left, right):
-        proj[part, rows, LEFT] = encode(left)
-        proj[part, rows, RIGHT] = encode(right)
+        proj[part, rows, LEFT] = encode_fine(left)
+        proj[part, rows, RIGHT] = encode_fine(right)
         gathers[part].stage0()
 
     run_reduces(reduces[0], reduces[1], done)
@@ -410,9 +423,9 @@
     whole = np.block([[cosines, -sines], [sines, cosines]]).astype(np.float32)
     high = whole.astype(jnp.bfloat16)
     low = (whole - high.astype(np.float32)).astype(jnp.bfloat16)
-    across = np.concatenate([high, high, low], axis=1)
-    across_t = np.concatenate([high.T, high.T, low.T], axis=1)
-    return across_t, np.ascontiguousarray(across_t.T), across, np.ascontiguousarray(across.T)
+    across = np.concatenate([high, high, low], axis=0)
+    down = np.concatenate([high.T, high.T, low.T], axis=1)
+    return [np.ascontiguousarray(t) for t in (down, across, high, high.T)]
 
 
 def split_join(values, axis):
@@ -421,94 +434,174 @@
     return jnp.concatenate([high, low, high], axis=axis)
 
 
+CHUNKS = 8
+CHUNK = GRID // CHUNKS
+
+
 def slots_kernel(
-    corners, count, proj, probe, diff, left_f, right_f, left_i, right_i,
-    image, probe_part, wide, total,
+    corners, count, proj, probe, diff, *refs,
 ):
-    slot = pl.program_id(0)
-
-    @pl.when(slot == 0)
-    def _():
+    tables, refs = refs[:4], refs[4:]
+    image, probe_part, proj_in, diff_in = refs[:4]
+    left_f, right_f, left_i, right_i, wide, total, image_out, in_sem, out_sem, sem = refs[4:]
+
+    def chunk_rows(k):
+        return pl.ds(pl.multiple_of(k * CHUNK, CHUNK), CHUNK)
+
+    def load(k):
+        rows = chunk_rows(k)
+        return pltpu.make_async_copy(proj.at[:, rows, :], proj_in.at[:, rows, :], in_sem.at[k])
+
+    def store(k):
+        rows = chunk_rows(k)
+        return pltpu.make_async_copy(image_out.at[:, rows, :], image.at[:, rows, :], out_sem.at[k])
+
+    for k in range(CHUNKS):
+        load(k).start()
+    later = [
+        pltpu.make_async_copy(src, dst, sem.at[k])
+        for k, (src, dst) in enumerate(
+            zip(tables + (diff,), (left_f, right_f, left_i, right_i, diff_in))
+        )
+    ]
+    for copy in later:
+        copy.start()
+    probe_part[...] = jnp.zeros(probe_part.shape, F32)
+
+    def open_chunk(k, carry):
+        rows = chunk_rows(k)
+        for tile in range(GRID // 128 + 1):
+            total[:, tile, rows, :] = jnp.zeros((2, CHUNK, 128), F32)
+        load(k).wait()
         for tile in range(GRID // 128):
-            wide[:, tile] = decode(proj[:, :, 128 * tile : 128 * tile + 128])
-        total[...] = jnp.zeros(total.shape, F32)
-        probe_part[...] = jnp.zeros(probe_part.shape, F32)
-
-    @pl.when(slot < count[0])
-    def _():
-        row = corners[slot, 0]
-        col = corners[slot, 1]
-        turn = lax.rem(col, 128)
-        tile = col // 128
-        lane = lax.broadcasted_iota(jnp.int32, (PATCH, 128), 1)
-        early = lane < turn
-        patch = []
-        for part in range(2):
-            window = [wide[part, tile + k, pl.ds(row, PATCH), :] for k in range(3)]
-            joined = jnp.concatenate([jnp.where(early, window[2], window[0]), window[1]], axis=1)
-            patch.append(pltpu.roll(joined, lax.rem(PATCH - turn, PATCH), 1))
-        patch_re, patch_im = patch
-        probe_re = probe[0]
-        probe_im = probe[1]
-        wave = jnp.concatenate(
+            wide[:, tile, rows, :] = decode_fine(proj_in[:, rows, 128 * tile : 128 * tile + 128])
+        return carry
+
+    lax.fori_loop(0, CHUNKS, open_chunk, 0)
+    for copy in later:
+        copy.wait()
+    live = count[0]
+    lane = lax.broadcasted_iota(jnp.int32, (PATCH, 128), 1)
+    zero = jnp.zeros((PATCH, 128), F32)
+    probe_re = probe[0]
+    probe_im = probe[1]
+
+    def pair_step(pair, carry):
+        waves = []
+        places = []
+        for k in range(2):
+            slot = 2 * pair + k
+            row = corners[slot, 0]
+            col = corners[slot, 1]
+            turn = lax.rem(col, 128)
+            tile = col // 128
+            early = lane < turn
+            patch = []
+            for part in range(2):
+                window = [wide[part, tile + m, pl.ds(row, PATCH), :] for m in range(3)]
+                joined = jnp.concatenate(
+                    [jnp.where(early, window[2], window[0]), window[1]], axis=1
+                )
+                patch.append(pltpu.roll(joined, lax.rem(PATCH - turn, PATCH), 1))
+            places.append((slot, row, turn, tile, early, patch))
+            waves.append(
+                jnp.concatenate(
+                    [
+                        probe_re * patch[0] - probe_im * patch[1],
+                        probe_re * patch[1] + probe_im * patch[0],
+                    ],
+                    axis=0,
+                )
+            )
+        half = dot(left_f[...], split_join(jnp.concatenate(waves, axis=1), 0))
+        half = jnp.concatenate(
             [
-                probe_re * patch_re - probe_im * patch_im,
-                probe_re * patch_im + probe_im * patch_re,
+                jnp.concatenate([half[:PATCH, cols], half[PATCH:, cols]], axis=1)
+                for cols in (slice(0, PATCH), slice(PATCH, 2 * PATCH))
             ],
             axis=0,
         )
-        half = dot(left_f[...], split_join(wave, 0))
-        half = jnp.concatenate([half[:PATCH], half[PATCH:]], axis=1)
         far = dot(split_join(half, 1), right_f[...])
-        far_re = far[:, :PATCH]
-        far_im = far[:, PATCH:]
-        misfit = (far_re * far_re + far_im * far_im - diff[0]) * (1.0 / math.sqrt(POSITIONS))
-        resid = jnp.concatenate([misfit * far_re, misfit * far_im], axis=0)
-        inner = dot(left_i[...], split_join(resid, 0))
-        inner = jnp.concatenate([inner[:PATCH], inner[PATCH:]], axis=1)
-        chi = dot(split_join(inner, 1), right_i[...])
-        chi_re = chi[:, :PATCH]
-        chi_im = chi[:, PATCH:]
-        probe_part[0] += patch_re * chi_re + patch_im * chi_im
-        probe_part[1] += patch_re * chi_im - patch_im * chi_re
-        grads = (
-            probe_re * chi_re + probe_im * chi_im,
-            probe_re * chi_im - probe_im * chi_re,
+        resid = []
+        for k in range(2):
+            slot = places[k][0]
+            far_re = far[PATCH * k : PATCH * k + PATCH, :PATCH]
+            far_im = far[PATCH * k : PATCH * k + PATCH, PATCH:]
+            weight = jnp.where(slot < live, 1.0 / math.sqrt(POSITIONS), 0.0)
+            misfit = (far_re * far_re + far_im * far_im - diff_in[slot]) * weight
+            resid.append(
+                jnp.concatenate(
+                    [(misfit * far_re).astype(BF16), (misfit * far_im).astype(BF16)], axis=0
+                )
+            )
+        inner = dot(left_i[...], jnp.concatenate(resid, axis=1)).astype(BF16)
+        inner = jnp.concatenate(
+            [
+                jnp.concatenate([inner[:PATCH, cols], inner[PATCH:, cols]], axis=1)
+                for cols in (slice(0, PATCH), slice(PATCH, 2 * PATCH))
+            ],
+            axis=0,
         )
-        zero = jnp.zeros((PATCH, 128), F32)
-        for part in range(2):
-            turned = pltpu.roll(grads[part], turn, 1)
-            head = turned[:, :128]
-            spread = (jnp.where(early, zero, head), turned[:, 128:], jnp.where(early, head, zero))
-            for k in range(3):
-                total[part, tile + k, pl.ds(row, PATCH), :] += spread[k]
-
-    @pl.when(slot == SLOTS - 1)
-    def _():
+        chi = dot(inner, right_i[...])
+        for k in range(2):
+            slot, row, turn, tile, early, patch = places[k]
+            chi_re = chi[PATCH * k : PATCH * k + PATCH, :PATCH]
+            chi_im = chi[PATCH * k : PATCH * k + PATCH, PATCH:]
+            probe_part[0] += patch[0] * chi_re + patch[1] * chi_im
+            probe_part[1] += patch[0] * chi_im - patch[1] * chi_re
+            grads = (
+                probe_re * chi_re + probe_im * chi_im,
+                probe_re * chi_im - probe_im * chi_re,
+            )
+            for part in range(2):
+                turned = pltpu.roll(grads[part], turn, 1)
+                head = turned[:, :128]
+                spread = (
+                    jnp.where(early, zero, head), turned[:, 128:], jnp.where(early, head, zero)
+                )
+                for m in range(3):
+                    total[part, tile + m, pl.ds(row, PATCH), :] += spread[m]
+        return carry
+
+    lax.fori_loop(0, (live + 1) // 2, pair_step, 0)
+
+    def close_chunk(k, carry):
+        rows = chunk_rows(k)
         for tile in range(GRID // 128):
-            image[:, :, 128 * tile : 128 * tile + 128] = encode(total[:, tile])
+            image_out[:, rows, 128 * tile : 128 * tile + 128] = encode(total[:, tile, rows, :])
+        store(k).start()
+        return carry
+
+    lax.fori_loop(0, CHUNKS, close_chunk, 0)
+    for k in range(CHUNKS):
+        store(k).wait()
 
 
 def slots(corners, count, proj, probe, diffraction):
     tables = [jnp.asarray(t) for t in dft_tables()]
     whole = pl.BlockSpec(memory_space=pltpu.VMEM)
     scalar = pl.BlockSpec(memory_space=pltpu.SMEM)
+    far = pl.BlockSpec(memory_space=pl.ANY)
+    dma = pltpu.SemaphoreType.DMA
     return pl.pallas_call(
         slots_kernel,
-        grid=(SLOTS,),
         out_shape=(
             jax.ShapeDtypeStruct((2, GRID, GRID), BF16),
             jax.ShapeDtypeStruct((2, PATCH, PATCH), F32),
         ),
-        in_specs=[
-            scalar, scalar, whole, whole,
-            pl.BlockSpec((1, PATCH, PATCH), lambda i: (i, 0, 0)),
-            whole, whole, whole, whole,
-        ],
-        out_specs=(whole, whole),
+        in_specs=[scalar, scalar, far, whole, far] + [far] * 4,
+        out_specs=(far, whole),
         scratch_shapes=[
+            pltpu.VMEM((2, GRID, GRID), BF16),
+            pltpu.VMEM((SLOTS, PATCH, PATCH), F32),
+            pltpu.VMEM((512, 1536), BF16),
+            pltpu.VMEM((1536, 512), BF16),
+            pltpu.VMEM((512, 512), BF16),
+            pltpu.VMEM((512, 512), BF16),
             pltpu.VMEM((2, GRID // 128 + 1, GRID, 128), F32),
             pltpu.VMEM((2, GRID // 128 + 1, GRID, 128), F32),
+            pltpu.VMEM((2, GRID, GRID), BF16),
+            dma((CHUNKS,)), dma((CHUNKS,)), dma((5,)),
         ],
         compiler_params=pltpu.CompilerParams(vmem_limit_bytes=VMEM_LIMIT),
         name="slots",
@@ -517,8 +610,8 @@
 
 def backward_kernel(
     image, par_all, probe_part, result, probe_out,
-    t0, t1, ext, padded, gbuf, cbuf, hbuf, bbuf, fin,
-    pbuf, pacc, pcore, py, pxl, psum, hs, hr, fs, fr, xs, xr,
+    t0, t1, ext, padded, gbuf, cbuf, hbuf, bbuf, xsend, xrecv, fin,
+    pcode, pbuf, pcore, py, pxl, psum, hs, hr, fs, fr, xs, xr,
     sends, recvs, fsend, frecv,
 ):
     place = Place()
@@ -532,9 +625,10 @@
     def ang_id(xl_, y_, core_):
         return (xl_ * 4 + y_) * 2 + core_
 
-    def chip_peer(j):
-        return (lax.rem(chip + j, 8) * 2 + core, me)
-
+    def y_peer(dy):
+        return (ang_id(xl, lax.rem(y + dy, 4), core), me)
+
+    xl_peer = (ang_id(1 - xl, y, core), me)
     core_peer = (ang_id(xl, y, 1 - core), me)
     turn_peer = (ang_id(xh, z, core), y * 2 + xl)
     stays = jnp.logical_and(xl == xh, y == z)
@@ -542,9 +636,8 @@
     below = (ang, slab_of(lax.rem(mine + 1, NSLAB)))
 
     barrier = greet(place)
-    for j in range(1, NSLAB):
-        pl.semaphore_signal(barrier, inc=1, device_id=chip_peer(j), device_id_type=MESH)
-    pl.semaphore_signal(barrier, inc=1, device_id=core_peer, device_id_type=MESH)
+    for peer in (y_peer(1), y_peer(2), y_peer(3), xl_peer, core_peer):
+        pl.semaphore_signal(barrier, inc=1, device_id=peer, device_id_type=MESH)
 
     @pl.when(jnp.logical_not(stays))
     def _():
@@ -562,7 +655,7 @@
     ext[:, HALO + ROWS + HALO :, :] = jnp.zeros((2, 384 - ROWS - 2 * HALO, GRID), BF16)
     padded[:, :PAD] = jnp.zeros((NSLAB * ROWS, PAD), BF16)
     padded[:, PAD + GRID :] = jnp.zeros((NSLAB * ROWS, PAD), BF16)
-    pl.semaphore_wait(barrier, 2 * (NSLAB - 1) + 1 + jnp.where(stays, 0, 1))
+    pl.semaphore_wait(barrier, NSLAB - 1 + 5 + jnp.where(stays, 0, 1))
 
     post = Post(sends, recvs)
     peers = [(dz, other) for dz in range(4) for other in range(2)][1:]
@@ -577,7 +670,7 @@
         def own(dz, other, lo, n, cols, part=part, ref=ref):
             return decode(ref(dz, other, lo, n, cols, None)[...])
 
-        reduces.append(Reduce(post, place, part, bufs, own, ref))
+        reduces.append(Reduce(post, place, part, bufs, own, ref, (encode, decode)))
     first, second = reduces
 
     def open_reduce(reduce):
@@ -597,7 +690,7 @@
             post.go(ext.at[part, pl.ds(ROWS, HALO), :], ext.at[part, pl.ds(0, HALO), :], below),
         ]
 
-    cores = {}
+    chips = {0: [], 1: []}
 
     def spread_slices(part):
         for copy in halos[part]:
@@ -615,7 +708,11 @@
             cols = pl.ds(256 * q, 256)
             padded[:, PAD + 256 * q : PAD + 256 * q + 256] = dot(t0[...], ext[part, :, cols]).astype(BF16)
 
-        def slice_step(s, carry):
+        cores = {}
+
+        def slice_step(j):
+            dy, other = j // 2, j % 2
+            s = lax.rem(y + dy, 4) * 2 + (1 - xl if other else xl)
             rows = pl.ds(pl.multiple_of(s * ROWS, ROWS), ROWS)
             stack = jnp.concatenate(
                 [padded[rows, 256 * q : 256 * q + 512] for q in range(GRID // 256)], axis=0
@@ -625,30 +722,25 @@
                 cols = slice(256 * q, 256 * q + 256)
                 for half in range(2):
                     lo = ROWS * q + HALF * half
-                    gbuf[part, half, s, :, cols] = tiles[lo : lo + HALF]
-            return carry
-
-        cores[part] = []
-        for k in range(2):
-            lax.fori_loop(4 * k, 4 * k + 4, slice_step, 0)
-            group = pl.ds(4 * k, 4)
-            cores[part].append(
-                post.go(gbuf.at[part, 1 - core, group], cbuf.at[part, group], core_peer)
-            )
-
-    chips = {}
-
-    def combine(part):
-        for copy in cores[part]:
-            copy.wait_recv()
-        chips[part] = []
-        for j in (4, 6, 2, 5, 7, 1, 3, 0):
-            target = lax.rem(chip + j, 8)
-            s = lax.rem(target, 4) * 2 + target // 4
-            both = decode(gbuf[part, core, s]) + decode(cbuf[part, s])
-            hbuf[part, j] = encode(both)
-            if j:
-                chips[part].append(post.go(hbuf.at[part, j], bbuf.at[part, j], chip_peer(j)))
+                    gbuf[part, half, j, :, cols] = tiles[lo : lo + HALF]
+            cores[j] = post.go(gbuf.at[part, 1 - core, j], cbuf.at[part, j], core_peer)
+
+        def combine(j):
+            cores[j].wait_recv()
+            dy, other = j // 2, j % 2
+            both = decode(gbuf[part, core, j]) + decode(cbuf[part, j])
+            hbuf[part, dy, other] = encode(both)
+            if dy:
+                span = hbuf.at[part, dy, other]
+                chips[part].append(post.go(span, bbuf.at[part, dy, other], y_peer(dy)))
+
+        order = (5, 4, 3, 7, 2, 6, 1, 0)
+        for k, j in enumerate(order):
+            slice_step(j)
+            if k >= 2:
+                combine(order[k - 2])
+        combine(order[-2])
+        combine(order[-1])
 
     def turn_copy(part):
         return pltpu.make_async_remote_copy(
@@ -656,13 +748,24 @@
             recv_sem=frecv.at[part], device_id=turn_peer, device_id_type=MESH,
         )
 
-    def settle(part):
+    sides = {}
+
+    def y_total(part, other):
+        total = decode(hbuf[part, 0, other])
+        for dy in range(1, 4):
+            total = total + decode(bbuf[part, dy, other])
+        return total
+
+    def settle_y(part):
         for copy in chips[part]:
             copy.wait_recv()
-        total = decode(hbuf[part, 0])
-        for j in range(1, NSLAB):
-            total = total + decode(bbuf[part, j])
-        fin[part] = encode(total)
+        xsend[part] = encode(y_total(part, 1))
+        sides[part] = post.go(xsend.at[part], xrecv.at[part], xl_peer)
+
+    def settle(part):
+        mine_total = y_total(part, 0)
+        sides[part].wait_recv()
+        fin[part] = encode(mine_total + decode(xrecv[part]))
 
         @pl.when(stays)
         def _():
@@ -673,15 +776,13 @@
             turn_copy(part).start()
 
     open_reduce(first)
+    first.stage1()
+    open_reduce(second)
+    pcode[...] = encode(probe_part[...])
     probe_copies = []
     for dz, other in peers:
-        dest = place.slab(dz, other)
-        rows = pl.ds(pl.multiple_of(dest * 64, 64), 64)
-        probe_copies.append(
-            post.go(probe_part.at[rows, :], pbuf.at[2 * dz + other], place.peer(dz, other))
-        )
-    first.stage1()
-    open_reduce(second)
+        rows = pl.ds(pl.multiple_of(place.slab(dz, other) * 64, 64), 64)
+        probe_copies.append(post.go(pcode.at[rows, :], pbuf.at[2 * dz + other], place.peer(dz, other)))
     first.stage2()
     first.stage3()
     first.stage4()
@@ -689,35 +790,34 @@
     second.stage2()
     finish_reduce(0, first)
     second.stage3()
+    second.stage4()
 
     total = probe_part[pl.ds(pl.multiple_of(me * 64, 64), 64), :]
     for copy, (dz, other) in zip(probe_copies, peers):
         copy.wait_recv()
-        total = total + pbuf[2 * dz + other]
-    pacc[...] = total
-    core_probe = post.go(pacc, pcore, core_peer)
-
-    second.stage4()
+        total = total + decode(pbuf[2 * dz + other])
+    psum[0] = encode(total)
+    core_probe = post.go(psum.at[0], pcore, core_peer)
+
     spread_slices(0)
+    core_probe.wait_recv()
+    psum[1] = encode(decode(psum[0]) + decode(pcore[...]))
+    y_copies = [
+        post.go(psum.at[1], py.at[j], y_peer(j)) for j in range(1, 4)
+    ]
     finish_reduce(1, second)
-
-    core_probe.wait_recv()
-    psum[0] = pacc[...] + pcore[...]
-    y_copies = [
-        post.go(psum.at[0], py.at[j], (ang_id(xl, lax.rem(y + j, 4), core), me)) for j in range(1, 4)
-    ]
-    combine(0)
-    spread_slices(1)
     for copy in y_copies:
         copy.wait_recv()
-    psum[1] = (psum[0] + py[1]) + (py[2] + py[3])
-    xl_probe = post.go(psum.at[1], pxl, (ang_id(1 - xl, y, core), me))
-    combine(1)
-    settle(0)
+    psum[2] = encode((decode(psum[1]) + decode(py[1])) + (decode(py[2]) + decode(py[3])))
+    xl_probe = post.go(psum.at[2], pxl, xl_peer)
+    spread_slices(1)
     xl_probe.wait_recv()
     span = probe_out.at[pl.ds(pl.multiple_of(me * 64, 64), 64), :]
-    span[...] = psum[1] + pxl[...]
+    span[...] = encode(decode(psum[2]) + decode(pxl[...]))
     out_copies = [post.go(span, span, place.peer(*peer)) for peer in peers]
+    settle_y(0)
+    settle(0)
+    settle_y(1)
     settle(1)
     for copy in out_copies:
         copy.wait_recv()
@@ -737,7 +837,7 @@
         backward_kernel,
         out_shape=(
             jax.ShapeDtypeStruct((2, HALF, GRID), BF16),
-            jax.ShapeDtypeStruct((2 * PATCH, PATCH), F32),
+            jax.ShapeDtypeStruct((2 * PATCH, PATCH), BF16),
         ),
         in_specs=[whole] * 3,
         out_specs=(whole, whole),
@@ -748,15 +848,17 @@
             pltpu.VMEM((NSLAB * ROWS, GRID + 2 * PAD), BF16),
             pltpu.VMEM((2, 2, NSLAB, HALF, GRID), BF16),
             pltpu.VMEM((2, NSLAB, HALF, GRID), BF16),
-            pltpu.VMEM((2, NSLAB, HALF, GRID), BF16),
-            pltpu.VMEM((2, NSLAB, HALF, GRID), BF16),
+            pltpu.VMEM((2, 4, 2, HALF, GRID), BF16),
+            pltpu.VMEM((2, 4, 2, HALF, GRID), BF16),
             pltpu.VMEM((2, HALF, GRID), BF16),
-            pltpu.VMEM((NSLAB, 64, PATCH), F32),
-            pltpu.VMEM((64, PATCH), F32),
-            pltpu.VMEM((64, PATCH), F32),
-            pltpu.VMEM((4, 64, PATCH), F32),
-            pltpu.VMEM((64, PATCH), F32),
-            pltpu.VMEM((2, 64, PATCH), F32),
+            pltpu.VMEM((2, HALF, GRID), BF16),
+            pltpu.VMEM((2, HALF, GRID), BF16),
+            pltpu.VMEM((2 * PATCH, PATCH), BF16),
+            pltpu.VMEM((NSLAB, 64, PATCH), BF16),
+            pltpu.VMEM((64, PATCH), BF16),
+            pltpu.VMEM((4, 64, PATCH), BF16),
+            pltpu.VMEM((64, PATCH), BF16),
+            pltpu.VMEM((3, 64, PATCH), BF16),
         ]
         + reduce_scratch()
         + [dma((96,)), dma((96,)), dma((2,)), dma((2,))],
@@ -782,7 +884,7 @@
     )
     result, probe_out = backward(image, par_all, probe_part.reshape(2 * PATCH, PATCH))
     object_grad = decode(jnp.transpose(result, (1, 0, 2)))[:, :, None, :]
-    return (object_grad, probe_out.reshape(2, PATCH, PATCH))
+    return (object_grad, decode(probe_out).reshape(2, PATCH, PATCH))
 
 
 def solution(mesh):

time: 217 us -> 199 us (0.917)
  the two profiles are of different devices: /device:TPU:66 before, /device:TPU:2 now
where the time goes in v2:
time: 199 us; the launch traced here: 196 us
  Pallas kernels  187 us (94%)
  other arithmetic  3.8 us (2%)
  local copies, waits for them, and re-layouts  3.66 us (2%)
    pallas_call x1, Pallas kernels, backward(): pl.pallas_call(backward_kernel, out_shape=(jax.ShapeDtypeStruct((2, HALF,...  98.2 us
    pallas_call x1, Pallas kernels, forward(): pl.pallas_call(forward_kernel, out_shape=(jax.ShapeDtypeStruct((2, GRID,...  73.8 us
    pallas_call x1, Pallas kernels, slots(): pl.pallas_call(slots_kernel, out_shape=(jax.ShapeDtypeStruct((2, GRID, GR...  15.4 us

profile of v2, /device:TPU:2, one launch (start us, length us, event | category | flops | bytes accessed | tf_op | source)
XLA Modules:
  0.0 196.2 jit_solution(8454165905625666614)
XLA Ops:
  0.6 0.0 copy-start
  1.3 0.0 copy-done
  1.3 0.2 dynamic-slice_reduce_fusion.offs
  1.5 0.0 copy-start.1
  1.5 0.8 convert_reduce_fusion
  2.4 0.1 reshape.23.wts
  2.4 0.0 copy-start.2
  2.4 0.1 pad_maximum_fusion
  2.5 1.3 copy.15.corners
  3.9 0.7 broadcast_in_dim.4.par
  4.6 0.0 copy-done.1
  4.6 0.0 copy-done.2
  4.6 73.8 %forward.1 = (bf16[2,1024,1024]{2,1,0:T(8,128)(2,1)}, f32[8,16,512]{2,1,0:T(8,128)}) custom-call(s32[2]{0:T(128)} %copy-done.1, f32[8]{0:T(128)} %copy-done.2, f32[16,512]{1,0:T(8,128)} %broadcast_in_dim.4.par, bf16[2,1024,1024]{2,1,0:T(8,128)(2,1)} %bitcast.20), custom_call_target="tpu_custom_call" | custom-call | tf_op jit(solution)/shard_map/forward/pallas_call | solution.py:382
  78.4 15.4 %slots.1 = (bf16[2,1024,1024]{2,1,0:T(8,128)(2,1)}, f32[2,256,256]{2,1,0:T(8,128)}) custom-call(s32[8,2]{1,0:T(8,128)} %copy.15.corners, s32[1]{0:T(128)} %bitcast.19.count, bf16[2,1024,1024]{2,1,0:T(8,128)(2,1)} %get-tuple-element.8.proj, f32[2,256,256]{2,1,0:T(8,128)} %probe.1, f32[8,256,256]{2,1,0:T(8,128)} %bitcast.21, ...), custom_call_target="tpu_custom_call" | custom-call | tf_op jit(solution)/shard_map/slots/pallas_call | solution.py:586
  93.8 98.2 %backward.1 = (bf16[2,64,1024]{2,1,0:T(8,128)(2,1)}, bf16[512,256]{1,0:T(8,128)(2,1)}) custom-call(bf16[2,1024,1024]{2,1,0:T(8,128)(2,1)} %get-tuple-element.9.image, f32[8,16,512]{2,1,0:T(8,128)} %get-tuple-element.10.par_all, f32[512,256]{1,0:T(8,128)} %bitcast.22), custom_call_target="tpu_custom_call" | custom-call | tf_op jit(solution)/shard_map/backward/pallas_call | solution.py:836
  192.0 1.0 fusion.4
  193.1 1.3 copy.16
  194.4 1.8 convert_multiply_fusion
  (2 shorter events, 0.0 us)
Async XLA Ops:
  0.6 0.7 copy-start
  1.5 3.1 %copy-start.1 = (s32[2]{0:T(128)}, s32[2]{0:T(128)S(1)}, u32[]{:S(2)}) copy-start(s32[2]{0:T(128)S(1)} %dynamic-slice_reduce_fusion.offs) | copy-start | bytes 28
  2.4 2.1 %copy-start.2 = (f32[8]{0:T(128)}, f32[8]{0:T(128)S(1)}, u32[]{:S(2)}) copy-start(f32[8]{0:T(128)S(1)} %reshape.23.wts) | copy-start | bytes 100

commit v3 on v2

--- a/solution.py
+++ b/solution.py
@@ -21,6 +21,7 @@
 PAD = 128
 HALO = 80
 POSITIONS = 512
+ANGLES = 16
 VMEM_LIMIT = 56 << 20
 
 
@@ -182,10 +183,6 @@
         src = self.ref(dz, 1, 0, ROWS, RIGHT, self.xs.at[dz])
         self.crossing[dz] = self.post.go(src, self.xr.at[dz], self.place.peer(0, 1))
 
-    def stage1(self):
-        self.rings[0].middle()
-        self.rings[1].middle()
-
     def stage2(self):
         self.crossing[2].wait_recv()
         self.rings[2].start()
@@ -284,25 +281,26 @@
     return barrier
 
 
-def run_reduces(first, second, done):
-    first.stage1()
-    second.stage1()
-    first.stage2()
-    first.stage3()
-    second.stage2()
-    first.stage4()
-    second.stage3()
-    left = first.stage5()
-    right = first.stage6()
-    done(0, left, right)
-    second.stage4()
-    left = second.stage5()
-    right = second.stage6()
-    done(1, left, right)
+def follow_reduces(reduces, done):
+    for reduce in reduces:
+        reduce.rings[0].middle()
+    for reduce in reduces:
+        reduce.stage2()
+        reduce.start_cross(1)
+        reduce.start_cross(3)
+    for reduce in reduces:
+        reduce.rings[1].middle()
+    for reduce in reduces:
+        reduce.stage3()
+    for reduce in reduces:
+        reduce.stage4()
+        reduce.start_cross(0)
+    for part, reduce in enumerate(reduces):
+        done(part, reduce.stage5(), reduce.stage6())
 
 
 def forward_kernel(
-    offs, wts, par, obj, proj, par_all,
+    offs, wts, obj, proj, par_all,
     opad, lift, t0, t1, dbuf, hs, hr, fs, fr, xs, xr,
     load_sem, sends, recvs,
 ):
@@ -314,13 +312,19 @@
     opad[:, PAD + GRID :, :] = jnp.zeros((2, PAD, GRID), BF16)
     lift[:, :PAD] = jnp.zeros((2 * ROWS, PAD), BF16)
     lift[:, PAD + GRID :] = jnp.zeros((2 * ROWS, PAD), BF16)
-    off_y = offs[0]
-    off_x = offs[1]
-    t0[...] = band(t0.shape, 0, (off_y + PAD - 1).astype(F32), [wts[t] for t in range(4)], 1)
-    t1[...] = band(t1.shape, 1, (off_x + PAD - 1).astype(F32), [wts[4 + t] for t in range(4)], 1)
+    ang = place.ang
+    off_y = offs[2 * ang].astype(F32)
+    off_x = offs[2 * ang + 1].astype(F32)
+    taps = [wts[8 * ang + k] for k in range(8)]
+    t0[...] = band(t0.shape, 0, off_y + float(PAD - 1), taps[:4], 1)
+    t1[...] = band(t1.shape, 1, off_x + float(PAD - 1), taps[4:], 1)
+    row_ids = lax.broadcasted_iota(jnp.int32, par_all.shape[1:], 0)
+    par = jnp.zeros(par_all.shape[1:], F32)
+    for k, value in enumerate(taps + [off_y, off_x]):
+        par = jnp.where(row_ids == k, value, par)
+    par_all[pl.ds(place.me, 1)] = par[None]
     load.wait()
 
-    par_all[pl.ds(place.me, 1)] = par[...][None]
     pl.semaphore_wait(barrier, NSLAB - 1)
     post = Post(sends, recvs)
     par_copies = []
@@ -359,8 +363,8 @@
         for reduce in reduces:
             if dz == 2:
                 reduce.start_far(other)
-            if other == 1:
-                reduce.start_cross(dz)
+                if other == 1:
+                    reduce.start_cross(2)
     rows = pl.ds(pl.multiple_of(place.block(0, 0) * ROWS, ROWS), ROWS)
     gathers = [Gather(post, place, part, proj) for part in range(2)]
 
@@ -369,7 +373,7 @@
         proj[part, rows, RIGHT] = encode_fine(right)
         gathers[part].stage0()
 
-    run_reduces(reduces[0], reduces[1], done)
+    follow_reduces(reduces, done)
     for k in range(1, 7):
         for gather in gathers:
             getattr(gather, "stage%d" % k)()
@@ -378,7 +382,7 @@
     post.finish()
 
 
-def forward(offs, wts, par, obj):
+def forward(offs, wts, obj):
     return pl.pallas_call(
         forward_kernel,
         out_shape=(
@@ -388,7 +392,6 @@
         in_specs=[
             pl.BlockSpec(memory_space=pltpu.SMEM),
             pl.BlockSpec(memory_space=pltpu.SMEM),
-            pl.BlockSpec(memory_space=pltpu.VMEM),
             pl.BlockSpec(memory_space=pl.ANY),
         ],
         out_specs=(
@@ -412,7 +415,7 @@
             collective_id=0, has_side_effects=True, vmem_limit_bytes=VMEM_LIMIT
         ),
         name="forward",
-    )(offs, wts, par, obj)
+    )(offs, wts, obj)
 
 
 def dft_tables():
@@ -491,8 +494,8 @@
         places = []
         for k in range(2):
             slot = 2 * pair + k
-            row = corners[slot, 0]
-            col = corners[slot, 1]
+            row = corners[2 * slot]
+            col = corners[2 * slot + 1]
             turn = lax.rem(col, 128)
             tile = col // 128
             early = lane < turn
@@ -610,8 +613,8 @@
 
 def backward_kernel(
     image, par_all, probe_part, result, probe_out,
-    t0, t1, ext, padded, gbuf, cbuf, hbuf, bbuf, xsend, xrecv, fin,
-    pcode, pbuf, pcore, py, pxl, psum, hs, hr, fs, fr, xs, xr,
+    t0, t1, ext, padded, gbuf, cbuf, yhs, yhr, yfs, yfr, xsend, xrecv, keep, fin, landed,
+    pcode, pall, pbuf, pcore, py, pxl, psum, hs, hr, fs, fr, xs, xr,
     sends, recvs, fsend, frecv,
 ):
     place = Place()
@@ -671,26 +674,22 @@
             return decode(ref(dz, other, lo, n, cols, None)[...])
 
         reduces.append(Reduce(post, place, part, bufs, own, ref, (encode, decode)))
-    first, second = reduces
-
-    def open_reduce(reduce):
-        for dz in (2, 1, 3, 0):
-            reduce.start_cross(dz)
-            if dz == 2:
-                reduce.start_far(1)
-                reduce.start_far(0)
-
     halos = {}
 
-    def finish_reduce(part, reduce):
-        ext[part, HALO : HALO + ROWS, LEFT] = reduce.stage5().astype(BF16)
-        ext[part, HALO : HALO + ROWS, RIGHT] = reduce.stage6().astype(BF16)
+    def done(part, left, right):
+        ext[part, HALO : HALO + ROWS, LEFT] = left.astype(BF16)
+        ext[part, HALO : HALO + ROWS, RIGHT] = right.astype(BF16)
         halos[part] = [
             post.go(ext.at[part, pl.ds(HALO, HALO), :], ext.at[part, pl.ds(HALO + ROWS, HALO), :], above),
             post.go(ext.at[part, pl.ds(ROWS, HALO), :], ext.at[part, pl.ds(0, HALO), :], below),
         ]
 
-    chips = {0: [], 1: []}
+    rings = {}
+
+    class YPlace:
+        @staticmethod
+        def peer(dy, other):
+            return y_peer(dy)
 
     def spread_slices(part):
         for copy in halos[part]:
@@ -725,72 +724,91 @@
                     gbuf[part, half, j, :, cols] = tiles[lo : lo + HALF]
             cores[j] = post.go(gbuf.at[part, 1 - core, j], cbuf.at[part, j], core_peer)
 
-        def combine(j):
-            cores[j].wait_recv()
-            dy, other = j // 2, j % 2
-            both = decode(gbuf[part, core, j]) + decode(cbuf[part, j])
-            hbuf[part, dy, other] = encode(both)
-            if dy:
-                span = hbuf.at[part, dy, other]
-                chips[part].append(post.go(span, bbuf.at[part, dy, other], y_peer(dy)))
-
-        order = (5, 4, 3, 7, 2, 6, 1, 0)
-        for k, j in enumerate(order):
-            slice_step(j)
-            if k >= 2:
-                combine(order[k - 2])
-        combine(order[-2])
-        combine(order[-1])
-
-    def turn_copy(part):
-        return pltpu.make_async_remote_copy(
-            src_ref=fin.at[part], dst_ref=result.at[part], send_sem=fsend.at[part],
-            recv_sem=frecv.at[part], device_id=turn_peer, device_id_type=MESH,
+        def arrived(*steps):
+            for j in steps:
+                cores[j].wait_recv()
+
+        def own(dy, lo, n):
+            both = [
+                decode(gbuf[part, core, j]) + decode(cbuf[part, j])
+                for j in range(2 * dy + lo // HALF, 2 * dy + (lo + n) // HALF)
+            ]
+            return both[0] if len(both) == 1 else jnp.concatenate(both, axis=0)
+
+        def far(k):
+            yhs[part, k] = encode(own(2, HALF * k, HALF))
+            return yhs.at[part, k]
+
+        ring = Ring(
+            post, YPlace, (yhr.at[part], yfs.at[part], yfr.at[part]), own, far, (encode, decode)
         )
+        slice_step(4)
+        slice_step(5)
+        slice_step(2)
+        arrived(4, 5)
+        ring.start()
+        slice_step(3)
+        slice_step(6)
+        slice_step(7)
+        arrived(2, 3, 6, 7)
+        ring.middle()
+        slice_step(0)
+        slice_step(1)
+        rings[part] = (ring, functools.partial(arrived, 0, 1))
 
     sides = {}
 
-    def y_total(part, other):
-        total = decode(hbuf[part, 0, other])
-        for dy in range(1, 4):
-            total = total + decode(bbuf[part, dy, other])
-        return total
-
     def settle_y(part):
-        for copy in chips[part]:
-            copy.wait_recv()
-        xsend[part] = encode(y_total(part, 1))
+        ring, ready = rings[part]
+        ready()
+        total = ring.end()
+        xsend[part] = encode(total[HALF:])
         sides[part] = post.go(xsend.at[part], xrecv.at[part], xl_peer)
+        keep[part] = total[:HALF]
 
     def settle(part):
-        mine_total = y_total(part, 0)
         sides[part].wait_recv()
-        fin[part] = encode(mine_total + decode(xrecv[part]))
+        fin[part] = encode(keep[part] + decode(xrecv[part]))
 
         @pl.when(stays)
         def _():
-            result[part] = fin[part]
+            landed[part] = fin[part]
 
         @pl.when(jnp.logical_not(stays))
         def _():
             turn_copy(part).start()
 
-    open_reduce(first)
-    first.stage1()
-    open_reduce(second)
+    def turn_copy(part):
+        return pltpu.make_async_remote_copy(
+            src_ref=fin.at[part], dst_ref=landed.at[part], send_sem=fsend.at[part],
+            recv_sem=frecv.at[part], device_id=turn_peer, device_id_type=MESH,
+        )
+
     pcode[...] = encode(probe_part[...])
     probe_copies = []
     for dz, other in peers:
         rows = pl.ds(pl.multiple_of(place.slab(dz, other) * 64, 64), 64)
         probe_copies.append(post.go(pcode.at[rows, :], pbuf.at[2 * dz + other], place.peer(dz, other)))
+    first, second = reduces
+
+    def open_reduce(reduce):
+        reduce.start_cross(2)
+        reduce.start_far(1)
+        reduce.start_far(0)
+
+    def more_cross(reduce):
+        reduce.start_cross(1)
+        reduce.start_cross(3)
+
+    open_reduce(first)
+    first.rings[0].middle()
+    open_reduce(second)
     first.stage2()
+    more_cross(first)
+    first.rings[1].middle()
+    first.start_cross(0)
     first.stage3()
-    first.stage4()
-    second.stage1()
-    second.stage2()
-    finish_reduce(0, first)
-    second.stage3()
-    second.stage4()
+    second.rings[0].middle()
 
     total = probe_part[pl.ds(pl.multiple_of(me * 64, 64), 64), :]
     for copy, (dz, other) in zip(probe_copies, peers):
@@ -799,22 +817,34 @@
     psum[0] = encode(total)
     core_probe = post.go(psum.at[0], pcore, core_peer)
 
-    spread_slices(0)
+    first.stage4()
+    second.stage2()
+    more_cross(second)
+    second.rings[1].middle()
+
     core_probe.wait_recv()
     psum[1] = encode(decode(psum[0]) + decode(pcore[...]))
-    y_copies = [
-        post.go(psum.at[1], py.at[j], y_peer(j)) for j in range(1, 4)
-    ]
-    finish_reduce(1, second)
+    y_copies = [post.go(psum.at[1], py.at[j], y_peer(j)) for j in range(1, 4)]
+
+    done(0, first.stage5(), first.stage6())
+    second.start_cross(0)
+    second.stage3()
+
     for copy in y_copies:
         copy.wait_recv()
     psum[2] = encode((decode(psum[1]) + decode(py[1])) + (decode(py[2]) + decode(py[3])))
     xl_probe = post.go(psum.at[2], pxl, xl_peer)
-    spread_slices(1)
+
+    second.stage4()
+    done(1, second.stage5(), second.stage6())
+    spread_slices(0)
+
     xl_probe.wait_recv()
-    span = probe_out.at[pl.ds(pl.multiple_of(me * 64, 64), 64), :]
+    span = pall.at[pl.ds(pl.multiple_of(me * 64, 64), 64), :]
     span[...] = encode(decode(psum[2]) + decode(pxl[...]))
     out_copies = [post.go(span, span, place.peer(*peer)) for peer in peers]
+
+    spread_slices(1)
     settle_y(0)
     settle(0)
     settle_y(1)
@@ -827,6 +857,9 @@
         turn_copy(0).wait()
         turn_copy(1).wait()
 
+    for part in range(2):
+        result[:, part, :] = decode(landed[part])
+    probe_out[...] = decode(pall[...])
     post.finish()
 
 
@@ -836,8 +869,8 @@
     return pl.pallas_call(
         backward_kernel,
         out_shape=(
-            jax.ShapeDtypeStruct((2, HALF, GRID), BF16),
-            jax.ShapeDtypeStruct((2 * PATCH, PATCH), BF16),
+            jax.ShapeDtypeStruct((HALF, 2, GRID), F32),
+            jax.ShapeDtypeStruct((2 * PATCH, PATCH), F32),
         ),
         in_specs=[whole] * 3,
         out_specs=(whole, whole),
@@ -848,11 +881,16 @@
             pltpu.VMEM((NSLAB * ROWS, GRID + 2 * PAD), BF16),
             pltpu.VMEM((2, 2, NSLAB, HALF, GRID), BF16),
             pltpu.VMEM((2, NSLAB, HALF, GRID), BF16),
-            pltpu.VMEM((2, 4, 2, HALF, GRID), BF16),
-            pltpu.VMEM((2, 4, 2, HALF, GRID), BF16),
+            pltpu.VMEM((2, 2, HALF, GRID), BF16),
+            pltpu.VMEM((2, 2, HALF, GRID), BF16),
+            pltpu.VMEM((2, 2, ROWS, GRID), BF16),
+            pltpu.VMEM((2, 2, ROWS, GRID), BF16),
             pltpu.VMEM((2, HALF, GRID), BF16),
             pltpu.VMEM((2, HALF, GRID), BF16),
+            pltpu.VMEM((2, HALF, GRID), F32),
             pltpu.VMEM((2, HALF, GRID), BF16),
+            pltpu.VMEM((2, HALF, GRID), BF16),
+            pltpu.VMEM((2 * PATCH, PATCH), BF16),
             pltpu.VMEM((2 * PATCH, PATCH), BF16),
             pltpu.VMEM((NSLAB, 64, PATCH), BF16),
             pltpu.VMEM((64, PATCH), BF16),
@@ -872,19 +910,16 @@
 def per_device(
     object_field, probe_field, diffraction, scan_offsets, counts, band_weights, band_offsets
 ):
-    ang = lax.axis_index("ang")
-    weights = lax.dynamic_index_in_dim(band_weights, ang, 0, keepdims=False)[0]
-    offsets = lax.dynamic_index_in_dim(band_offsets, ang, 0, keepdims=False)[0]
-    weights = weights.astype(F32).reshape(8)
-    par = jnp.concatenate([weights, offsets.astype(F32), jnp.zeros((6,), F32)])
-    par = jnp.broadcast_to(par[:, None], (16, 512))
-    proj, par_all = forward(offsets, weights, par, object_field.reshape(2, GRID, GRID))
+    proj, par_all = forward(
+        band_offsets.reshape(2 * ANGLES),
+        band_weights.astype(F32).reshape(8 * ANGLES),
+        object_field.reshape(2, GRID, GRID),
+    )
     image, probe_part = slots(
-        scan_offsets[0, 0], counts[0], proj, probe_field, diffraction[0, 0]
+        scan_offsets.reshape(2 * SLOTS), counts[0], proj, probe_field, diffraction[0, 0]
     )
     result, probe_out = backward(image, par_all, probe_part.reshape(2 * PATCH, PATCH))
-    object_grad = decode(jnp.transpose(result, (1, 0, 2)))[:, :, None, :]
-    return (object_grad, decode(probe_out).reshape(2, PATCH, PATCH))
+    return (result[:, :, None, :], probe_out.reshape(2, PATCH, PATCH))
 
 
 def solution(mesh):

time: 199 us -> 193 us (0.970); the launches traced: 196 us -> 192 us
  local copies, waits for them, and re-layouts: 3.66 us -> 8.41 us
  Pallas kernels: 187 us -> 183 us
  other arithmetic: 3.8 us -> 0 us
    pallas_call x1, Pallas kernels: 98.2 us -> 89.7 us  [backward(): pl.pallas_call(backward_kernel, out_shape=(jax.ShapeDtypeStruct((HALF, 2,...]
    pallas_call x1, Pallas kernels: 15.4 us -> 22 us  [slots(): pl.pallas_call(slots_kernel, out_shape=(jax.ShapeDtypeStruct((2, GRID, GR...]
    unnamed x7 -> x4, local copies, waits for them, and re-layouts: 1.36 us -> 5.75 us
    pallas_call x1, Pallas kernels: 73.8 us -> 71 us  [forward(): pl.pallas_call(forward_kernel, out_shape=(jax.ShapeDtypeStruct((2, GRID,...]
    reshape x0 -> x4, local copies, waits for them, and re-layouts: none -> 2.66 us  [the longest x2 1.47 us: per_device(): band_weights.astype(F32).reshape(8 * ANGLES)]
where the time goes in v3:
time: 193 us; the launch traced here: 192 us
  Pallas kernels  183 us (95%)
  local copies, waits for them, and re-layouts  8.41 us (4%)
    pallas_call x1, Pallas kernels, backward(): pl.pallas_call(backward_kernel, out_shape=(jax.ShapeDtypeStruct((HALF, 2,...  89.7 us
    pallas_call x1, Pallas kernels, forward(): pl.pallas_call(forward_kernel, out_shape=(jax.ShapeDtypeStruct((2, GRID,...  71 us
    pallas_call x1, Pallas kernels, slots(): pl.pallas_call(slots_kernel, out_shape=(jax.ShapeDtypeStruct((2, GRID, GR...  22 us
    unnamed x4, local copies, waits for them, and re-layouts  5.75 us

profile of v3, /device:TPU:2, one launch (start us, length us, event | category | flops | bytes accessed | tf_op | source)
XLA Modules:
  0.0 192.4 jit_solution(101916693383437591)
XLA Ops:
  1.3 0.8 copy.17
  2.0 0.6 reshape.24.corners
  2.6 0.8 copy.18
  3.4 0.6 reshape.25.offs
  4.0 0.8 copy.19
  4.8 0.7 reshape.32.wts
  5.5 71.0 %forward.1 = (bf16[2,1024,1024]{2,1,0:T(8,128)(2,1)}, f32[8,16,512]{2,1,0:T(8,128)}) custom-call(s32[32]{0:T(128)} %reshape.25.offs, f32[128]{0:T(128)} %reshape.32.wts, bf16[2,1024,1024]{2,1,0:T(8,128)(2,1)} %bitcast.13), custom_call_target="tpu_custom_call" | custom-call | tf_op jit(solution)/shard_map/forward/pallas_call | solution.py:386
  76.5 22.0 %slots.1 = (bf16[2,1024,1024]{2,1,0:T(8,128)(2,1)}, f32[2,256,256]{2,1,0:T(8,128)}) custom-call(s32[16]{0:T(128)} %reshape.24.corners, s32[1]{0:T(128)} %bitcast.12.count, bf16[2,1024,1024]{2,1,0:T(8,128)(2,1)} %get-tuple-element.8.proj, f32[2,256,256]{2,1,0:T(8,128)} %probe.1, f32[8,256,256]{2,1,0:T(8,128)} %bitcast.14, ...), custom_call_target="tpu_custom_call" | custom-call | tf_op jit(solution)/shard_map/slots/pallas_call | solution.py:589
  98.5 89.7 %backward.1 = (f32[64,2,1024]{2,1,0:T(2,128)}, f32[512,256]{1,0:T(8,128)}) custom-call(bf16[2,1024,1024]{2,1,0:T(8,128)(2,1)} %get-tuple-element.9.image, f32[8,16,512]{2,1,0:T(8,128)} %get-tuple-element.10.par_all, f32[512,256]{1,0:T(8,128)} %bitcast.15), custom_call_target="tpu_custom_call" | custom-call | tf_op jit(solution)/shard_map/backward/pallas_call | solution.py:869
  188.2 2.4 %copy.20 = f32[64,2,1,1024]{3,2,1,0:T(1,128)} copy(f32[64,2,1,1024]{3,1,0,2:T(2,128)} %bitcast.17) | data formatting | bytes 1048576
  190.5 1.9 copy.23

commit v4 on v3

--- a/solution.py
+++ b/solution.py
@@ -21,7 +21,6 @@
 PAD = 128
 HALO = 80
 POSITIONS = 512
-ANGLES = 16
 VMEM_LIMIT = 56 << 20
 
 
@@ -313,9 +312,9 @@
     lift[:, :PAD] = jnp.zeros((2 * ROWS, PAD), BF16)
     lift[:, PAD + GRID :] = jnp.zeros((2 * ROWS, PAD), BF16)
     ang = place.ang
-    off_y = offs[2 * ang].astype(F32)
-    off_x = offs[2 * ang + 1].astype(F32)
-    taps = [wts[8 * ang + k] for k in range(8)]
+    off_y = offs[ang, 0, 0].astype(F32)
+    off_x = offs[ang, 0, 1].astype(F32)
+    taps = [wts[ang, 0, k // 4, k % 4] for k in range(8)]
     t0[...] = band(t0.shape, 0, off_y + float(PAD - 1), taps[:4], 1)
     t1[...] = band(t1.shape, 1, off_x + float(PAD - 1), taps[4:], 1)
     row_ids = lax.broadcasted_iota(jnp.int32, par_all.shape[1:], 0)
@@ -483,7 +482,7 @@
     lax.fori_loop(0, CHUNKS, open_chunk, 0)
     for copy in later:
         copy.wait()
-    live = count[0]
+    live = count[0, 0]
     lane = lax.broadcasted_iota(jnp.int32, (PATCH, 128), 1)
     zero = jnp.zeros((PATCH, 128), F32)
     probe_re = probe[0]
@@ -494,8 +493,8 @@
         places = []
         for k in range(2):
             slot = 2 * pair + k
-            row = corners[2 * slot]
-            col = corners[2 * slot + 1]
+            row = corners[0, 0, slot, 0]
+            col = corners[0, 0, slot, 1]
             turn = lax.rem(col, 128)
             tile = col // 128
             early = lane < turn
@@ -613,7 +612,7 @@
 
 def backward_kernel(
     image, par_all, probe_part, result, probe_out,
-    t0, t1, ext, padded, gbuf, cbuf, yhs, yhr, yfs, yfr, xsend, xrecv, keep, fin, landed,
+    t0, t1, ext, padded, gbuf, cbuf, yhs, yhr, yfs, yfr, xsend, xrecv, keep, fin,
     pcode, pall, pbuf, pcore, py, pxl, psum, hs, hr, fs, fr, xs, xr,
     sends, recvs, fsend, frecv,
 ):
@@ -772,7 +771,7 @@
 
         @pl.when(stays)
         def _():
-            landed[part] = fin[part]
+            result[part] = fin[part]
 
         @pl.when(jnp.logical_not(stays))
         def _():
@@ -780,7 +779,7 @@
 
     def turn_copy(part):
         return pltpu.make_async_remote_copy(
-            src_ref=fin.at[part], dst_ref=landed.at[part], send_sem=fsend.at[part],
+            src_ref=fin.at[part], dst_ref=result.at[part], send_sem=fsend.at[part],
             recv_sem=frecv.at[part], device_id=turn_peer, device_id_type=MESH,
         )
 
@@ -857,8 +856,6 @@
         turn_copy(0).wait()
         turn_copy(1).wait()
 
-    for part in range(2):
-        result[:, part, :] = decode(landed[part])
     probe_out[...] = decode(pall[...])
     post.finish()
 
@@ -869,7 +866,7 @@
     return pl.pallas_call(
         backward_kernel,
         out_shape=(
-            jax.ShapeDtypeStruct((HALF, 2, GRID), F32),
+            jax.ShapeDtypeStruct((2, HALF, GRID), BF16),
             jax.ShapeDtypeStruct((2 * PATCH, PATCH), F32),
         ),
         in_specs=[whole] * 3,
@@ -889,7 +886,6 @@
             pltpu.VMEM((2, HALF, GRID), BF16),
             pltpu.VMEM((2, HALF, GRID), F32),
             pltpu.VMEM((2, HALF, GRID), BF16),
-            pltpu.VMEM((2, HALF, GRID), BF16),
             pltpu.VMEM((2 * PATCH, PATCH), BF16),
             pltpu.VMEM((2 * PATCH, PATCH), BF16),
             pltpu.VMEM((NSLAB, 64, PATCH), BF16),
@@ -911,15 +907,16 @@
     object_field, probe_field, diffraction, scan_offsets, counts, band_weights, band_offsets
 ):
     proj, par_all = forward(
-        band_offsets.reshape(2 * ANGLES),
-        band_weights.astype(F32).reshape(8 * ANGLES),
+        band_offsets,
+        band_weights.astype(F32),
         object_field.reshape(2, GRID, GRID),
     )
     image, probe_part = slots(
-        scan_offsets.reshape(2 * SLOTS), counts[0], proj, probe_field, diffraction[0, 0]
+        scan_offsets, counts, proj, probe_field, diffraction[0, 0]
     )
     result, probe_out = backward(image, par_all, probe_part.reshape(2 * PATCH, PATCH))
-    return (result[:, :, None, :], probe_out.reshape(2, PATCH, PATCH))
+    object_grad = decode(jnp.transpose(result, (1, 0, 2)))[:, :, None, :]
+    return (object_grad, probe_out.reshape(2, PATCH, PATCH))
 
 
 def solution(mesh):

time: 193 us -> 190 us (0.984); the launches traced: 192 us -> 187 us
  Pallas kernels: 183 us -> 177 us
    pallas_call x1, Pallas kernels: 22 us -> 12 us  [slots(): pl.pallas_call(slots_kernel, out_shape=(jax.ShapeDtypeStruct((2, GRID, GR...]
    pallas_call x1, Pallas kernels: 89.7 us -> 93.9 us  [backward(): pl.pallas_call(backward_kernel, out_shape=(jax.ShapeDtypeStruct((2, HALF,...]
    reshape x4 -> x0, local copies, waits for them, and re-layouts: 2.66 us -> none  [the longest x2 1.47 us: per_device(): band_weights.astype(F32).reshape(8 * ANGLES)]
where the time goes in v4:
time: 190 us; the launch traced here: 187 us
  Pallas kernels  177 us (93%)
  local copies, waits for them, and re-layouts  7.27 us (4%)
    pallas_call x1, Pallas kernels, backward(): pl.pallas_call(backward_kernel, out_shape=(jax.ShapeDtypeStruct((2, HALF,...  93.9 us
    pallas_call x1, Pallas kernels, forward(): pl.pallas_call(forward_kernel, out_shape=(jax.ShapeDtypeStruct((2, GRID,...  71.4 us
    pallas_call x1, Pallas kernels, slots(): pl.pallas_call(slots_kernel, out_shape=(jax.ShapeDtypeStruct((2, GRID, GR...  12 us
    unnamed x4, local copies, waits for them, and re-layouts  5.9 us

profile of v4, /device:TPU:2, one launch (start us, length us, event | category | flops | bytes accessed | tf_op | source)
XLA Modules:
  0.0 187.0 jit_solution(2456206553749283398)
XLA Ops:
  1.3 1.3 copy.19.corners
  2.6 1.4 copy.17.offs
  4.0 1.4 copy.18.wts
  5.4 71.4 %forward.1 = (bf16[2,1024,1024]{2,1,0:T(8,128)(2,1)}, f32[8,16,512]{2,1,0:T(8,128)}) custom-call(s32[16,1,2]{2,1,0:T(1,128)} %copy.17.offs, f32[16,1,2,4]{3,2,1,0:T(2,128)} %copy.18.wts, bf16[2,1024,1024]{2,1,0:T(8,128)(2,1)} %bitcast.17), custom_call_target="tpu_custom_call" | custom-call | tf_op jit(solution)/shard_map/forward/pallas_call | solution.py:385
  76.8 12.0 %slots.1 = (bf16[2,1024,1024]{2,1,0:T(8,128)(2,1)}, f32[2,256,256]{2,1,0:T(8,128)}) custom-call(s32[1,1,8,2]{3,2,1,0:T(8,128)} %copy.19.corners, s32[1,1]{1,0:T(1,128)S(6)} %copy.22.count, bf16[2,1024,1024]{2,1,0:T(8,128)(2,1)} %get-tuple-element.8.proj, f32[2,256,256]{2,1,0:T(8,128)} %probe.1, f32[8,256,256]{2,1,0:T(8,128)} %bitcast.18, ...), custom_call_target="tpu_custom_call" | custom-call | tf_op jit(solution)/shard_map/slots/pallas_call | solution.py:588
  88.8 93.9 %backward.1 = (bf16[2,64,1024]{2,1,0:T(8,128)(2,1)}, f32[512,256]{1,0:T(8,128)}) custom-call(bf16[2,1024,1024]{2,1,0:T(8,128)(2,1)} %get-tuple-element.9.image, f32[8,16,512]{2,1,0:T(8,128)} %get-tuple-element.10.par_all, f32[512,256]{1,0:T(8,128)} %bitcast.19), custom_call_target="tpu_custom_call" | custom-call | tf_op jit(solution)/shard_map/backward/pallas_call | solution.py:866
  182.7 1.0 fusion.2
  183.8 1.3 copy.20
  185.1 1.9 copy.23

commit v5 on v4

--- a/solution.py
+++ b/solution.py
@@ -311,10 +311,9 @@
     opad[:, PAD + GRID :, :] = jnp.zeros((2, PAD, GRID), BF16)
     lift[:, :PAD] = jnp.zeros((2 * ROWS, PAD), BF16)
     lift[:, PAD + GRID :] = jnp.zeros((2 * ROWS, PAD), BF16)
-    ang = place.ang
-    off_y = offs[ang, 0, 0].astype(F32)
-    off_x = offs[ang, 0, 1].astype(F32)
-    taps = [wts[ang, 0, k // 4, k % 4] for k in range(8)]
+    off_y = offs[0].astype(F32)
+    off_x = offs[1].astype(F32)
+    taps = [wts[k] for k in range(8)]
     t0[...] = band(t0.shape, 0, off_y + float(PAD - 1), taps[:4], 1)
     t1[...] = band(t1.shape, 1, off_x + float(PAD - 1), taps[4:], 1)
     row_ids = lax.broadcasted_iota(jnp.int32, par_all.shape[1:], 0)
@@ -906,9 +905,12 @@
 def per_device(
     object_field, probe_field, diffraction, scan_offsets, counts, band_weights, band_offsets
 ):
+    ang = lax.axis_index("ang")
+    weights = lax.dynamic_index_in_dim(band_weights, ang, 0, keepdims=False)[0]
+    offsets = lax.dynamic_index_in_dim(band_offsets, ang, 0, keepdims=False)[0]
     proj, par_all = forward(
-        band_offsets,
-        band_weights.astype(F32),
+        offsets,
+        weights.astype(F32).reshape(8),
         object_field.reshape(2, GRID, GRID),
     )
     image, probe_part = slots(

time: 190 us -> 192 us (1.011); the launches traced: 187 us -> 191 us
  Pallas kernels: 177 us -> 182 us
    pallas_call x1, Pallas kernels: 93.9 us -> 99.2 us  [backward(): pl.pallas_call(backward_kernel, out_shape=(jax.ShapeDtypeStruct((2, HALF,...]
    unnamed x4 -> x5, local copies, waits for them, and re-layouts: 5.9 us -> 4.56 us
where the time goes in v5:
time: 192 us; the launch traced here: 191 us
  Pallas kernels  182 us (95%)
  local copies, waits for them, and re-layouts  5.93 us (3%)
    pallas_call x1, Pallas kernels, backward(): pl.pallas_call(backward_kernel, out_shape=(jax.ShapeDtypeStruct((2, HALF,...  99.2 us
    pallas_call x1, Pallas kernels, forward(): pl.pallas_call(forward_kernel, out_shape=(jax.ShapeDtypeStruct((2, GRID,...  71 us
    pallas_call x1, Pallas kernels, slots(): pl.pallas_call(slots_kernel, out_shape=(jax.ShapeDtypeStruct((2, GRID, GR...  12.1 us
    unnamed x5, local copies, waits for them, and re-layouts  4.56 us

profile of v5, /device:TPU:2, one launch (start us, length us, event | category | flops | bytes accessed | tf_op | source)
XLA Modules:
  0.0 191.4 jit_solution(2820492900176822029)
XLA Ops:
  0.6 0.0 copy-start
  1.3 0.0 copy-done
  1.3 0.7 dynamic-slice_reduce_fusion.offs
  2.0 0.8 convert_reduce_fusion
  2.9 0.7 reshape.22.wts
  3.5 1.3 copy.15.corners
  4.9 71.0 %forward.1 = (bf16[2,1024,1024]{2,1,0:T(8,128)(2,1)}, f32[8,16,512]{2,1,0:T(8,128)}) custom-call(s32[2]{0:T(128)} %dynamic-slice_reduce_fusion.offs, f32[8]{0:T(128)} %reshape.22.wts, bf16[2,1024,1024]{2,1,0:T(8,128)(2,1)} %bitcast.17), custom_call_target="tpu_custom_call" | custom-call | tf_op jit(solution)/shard_map/forward/pallas_call | solution.py:384
  75.9 12.1 %slots.1 = (bf16[2,1024,1024]{2,1,0:T(8,128)(2,1)}, f32[2,256,256]{2,1,0:T(8,128)}) custom-call(s32[1,1,8,2]{3,2,1,0:T(8,128)} %copy.15.corners, s32[1,1]{1,0:T(1,128)S(6)} %copy.18.count, bf16[2,1024,1024]{2,1,0:T(8,128)(2,1)} %get-tuple-element.8.proj, f32[2,256,256]{2,1,0:T(8,128)} %probe.1, f32[8,256,256]{2,1,0:T(8,128)} %bitcast.18, ...), custom_call_target="tpu_custom_call" | custom-call | tf_op jit(solution)/shard_map/slots/pallas_call | solution.py:587
  88.0 99.2 %backward.1 = (bf16[2,64,1024]{2,1,0:T(8,128)(2,1)}, f32[512,256]{1,0:T(8,128)}) custom-call(bf16[2,1024,1024]{2,1,0:T(8,128)(2,1)} %get-tuple-element.9.image, f32[8,16,512]{2,1,0:T(8,128)} %get-tuple-element.10.par_all, f32[512,256]{1,0:T(8,128)} %bitcast.19), custom_call_target="tpu_custom_call" | custom-call | tf_op jit(solution)/shard_map/backward/pallas_call | solution.py:865
  187.1 1.0 fusion.2
  188.2 1.3 copy.16
  189.5 1.9 copy.19
Async XLA Ops:
  0.6 0.7 copy-start

commit v6 on v5

--- a/solution.py
+++ b/solution.py
@@ -21,7 +21,6 @@
 PAD = 128
 HALO = 80
 POSITIONS = 512
-VMEM_LIMIT = 56 << 20
 
 
 def block_of(slab):
@@ -410,7 +409,7 @@
             pltpu.SemaphoreType.DMA((96,)),
         ],
         compiler_params=pltpu.CompilerParams(
-            collective_id=0, has_side_effects=True, vmem_limit_bytes=VMEM_LIMIT
+            collective_id=0, has_side_effects=True, vmem_limit_bytes=34 << 20
         ),
         name="forward",
     )(offs, wts, obj)
@@ -604,7 +603,7 @@
             pltpu.VMEM((2, GRID, GRID), BF16),
             dma((CHUNKS,)), dma((CHUNKS,)), dma((5,)),
         ],
-        compiler_params=pltpu.CompilerParams(vmem_limit_bytes=VMEM_LIMIT),
+        compiler_params=pltpu.CompilerParams(vmem_limit_bytes=44 << 20),
         name="slots",
     )(corners, count, proj, probe, diffraction, *tables)
 
@@ -896,7 +895,7 @@
         + reduce_scratch()
         + [dma((96,)), dma((96,)), dma((2,)), dma((2,))],
         compiler_params=pltpu.CompilerParams(
-            collective_id=1, has_side_effects=True, vmem_limit_bytes=VMEM_LIMIT
+            collective_id=1, has_side_effects=True, vmem_limit_bytes=38 << 20
         ),
         name="backward",
     )(image, par_all, probe_part)

time: 192 us -> 188 us (0.979)
  the two profiles are of different devices: /device:TPU:2 before, /device:TPU:30 now
where the time goes in v6:
time: 188 us; the launch traced here: 185 us
  Pallas kernels  170 us (90%)
  local copies, waits for them, and re-layouts  13 us (7%)
    pallas_call x1, Pallas kernels, backward(): pl.pallas_call(backward_kernel, out_shape=(jax.ShapeDtypeStruct((2, HALF,...  80.2 us
    pallas_call x1, Pallas kernels, forward(): pl.pallas_call(forward_kernel, out_shape=(jax.ShapeDtypeStruct((2, GRID,...  68.8 us
    pallas_call x1, Pallas kernels, slots(): pl.pallas_call(slots_kernel, out_shape=(jax.ShapeDtypeStruct((2, GRID, GR...  21.1 us
    unnamed x23, local copies, waits for them, and re-layouts  12.7 us

profile of v6, /device:TPU:30, one launch (start us, length us, event | category | flops | bytes accessed | tf_op | source)
XLA Modules:
  0.0 185.4 jit_solution(6445276524782626426)
XLA Ops:
  0.6 0.0 copy-start
  1.3 0.0 copy-done
  1.3 0.2 dynamic-slice_reduce_fusion.offs
  1.5 0.8 convert_reduce_fusion
  2.3 0.1 reshape.22.wts
  2.4 0.8 copy.15.corners
  3.2 0.0 copy-start.1
  3.2 2.2 %copy-done.1 = bf16[2,1,1024,1024]{3,2,1,0:T(8,128)(2,1)S(1)} copy-done((bf16[2,1,1024,1024]{3,2,1,0:T(8,128)(2,1)S(1)}, bf16[2,1,1024,1024]{3,2,1,0:T(8,128)(2,1)}, u32[]{:S(2)}) %copy-start.1) | copy-done | bytes 4194328
  5.4 0.0 copy-start.4
  5.4 0.0 copy-start.5
  5.4 0.0 copy-start.7
  5.4 68.8 %forward.1 = (bf16[2,1024,1024]{2,1,0:T(8,128)(2,1)S(1)}, f32[8,16,512]{2,1,0:T(8,128)S(1)}) custom-call(s32[2]{0:T(128)S(1)} %dynamic-slice_reduce_fusion.offs, f32[8]{0:T(128)S(1)} %reshape.22.wts, bf16[2,1024,1024]{2,1,0:T(8,128)(2,1)S(1)} %bitcast.17), custom_call_target="tpu_custom_call" | custom-call | tf_op jit(solution)/shard_map/forward/pallas_call | solution.py:383
  74.2 0.0 copy-start.3
  74.2 1.9 %copy-done.3 = bf16[2,1024,1024]{2,1,0:T(8,128)(2,1)} copy-done((bf16[2,1024,1024]{2,1,0:T(8,128)(2,1)}, bf16[2,1024,1024]{2,1,0:T(8,128)(2,1)S(1)}, u32[]{:S(2)}) %copy-start.3) | copy-done | bytes 4194328
  76.2 0.0 copy-done.4
  76.2 0.0 copy-done.5
  76.2 0.0 copy-done.7
  76.2 0.0 copy-start.6
  76.2 1.4 copy-done.6
  77.6 0.0 copy-start.8
  77.6 1.0 copy-done.8
  78.6 0.0 copy-start.9
  78.6 1.0 copy-done.9
  79.7 21.1 %slots.1 = (bf16[2,1024,1024]{2,1,0:T(8,128)(2,1)}, f32[2,256,256]{2,1,0:T(8,128)S(1)}) custom-call(s32[1,1,8,2]{3,2,1,0:T(8,128)S(1)} %copy.15.corners, s32[1,1]{1,0:T(1,128)S(6)} %copy.18.count, bf16[2,1024,1024]{2,1,0:T(8,128)(2,1)} %copy-done.3, f32[2,256,256]{2,1,0:T(8,128)S(1)} %copy-done.7, f32[8,256,256]{2,1,0:T(8,128)S(1)} %bitcast.18, ...), custom_call_target="tpu_custom_call" | custom-call | tf_op jit(solution)/shard_map/slots/pallas_call | solution.py:586
  100.8 0.0 copy-start.2
  100.8 2.2 %copy-done.2 = bf16[2,1024,1024]{2,1,0:T(8,128)(2,1)S(1)} copy-done((bf16[2,1024,1024]{2,1,0:T(8,128)(2,1)S(1)}, bf16[2,1024,1024]{2,1,0:T(8,128)(2,1)}, u32[]{:S(2)}) %copy-start.2) | copy-done | bytes 4194328
  103.0 80.2 %backward.1 = (bf16[2,64,1024]{2,1,0:T(8,128)(2,1)S(1)}, f32[512,256]{1,0:T(8,128)S(1)}) custom-call(bf16[2,1024,1024]{2,1,0:T(8,128)(2,1)S(1)} %copy-done.2, f32[8,16,512]{2,1,0:T(8,128)S(1)} %get-tuple-element.10.par_all, f32[512,256]{1,0:T(8,128)S(1)} %bitcast.19), custom_call_target="tpu_custom_call" | custom-call | tf_op jit(solution)/shard_map/backward/pallas_call | solution.py:864
  183.2 0.1 fusion.2
  183.3 1.3 copy.16
  184.6 0.8 copy.19
Async XLA Ops:
  0.6 0.7 copy-start
  3.2 2.2 %copy-start.1 = (bf16[2,1,1024,1024]{3,2,1,0:T(8,128)(2,1)S(1)}, bf16[2,1,1024,1024]{3,2,1,0:T(8,128)(2,1)}, u32[]{:S(2)}) copy-start(bf16[2,1,1024,1024]{3,2,1,0:T(8,128)(2,1)} %param.11) | copy-start | bytes 12582916
  5.4 70.8 %copy-start.4 = (f32[1,1,8,256,256]{4,3,2,1,0:T(8,128)S(1)}, f32[1,1,8,256,256]{4,3,2,1,0:T(8,128)}, u32[]{:S(2)}) copy-start(f32[1,1,8,256,256]{4,3,2,1,0:T(8,128)} %param.13) | copy-start | bytes 6291460
  5.4 70.8 %copy-start.5 = (bf16[1536,512]{1,0:T(8,128)(2,1)S(1)}, bf16[1536,512]{1,0:T(8,128)(2,1)}, u32[]{:S(2)}) copy-start(bf16[1536,512]{1,0:T(8,128)(2,1)} %constant.27.clone.refs_1_) | copy-start | bytes 4718596
  5.4 70.8 %copy-start.7 = (f32[2,256,256]{2,1,0:T(8,128)S(1)}, f32[2,256,256]{2,1,0:T(8,128)}, u32[]{:S(2)}) copy-start(f32[2,256,256]{2,1,0:T(8,128)} %probe.1) | copy-start | bytes 1572868
  74.2 1.9 %copy-start.3 = (bf16[2,1024,1024]{2,1,0:T(8,128)(2,1)}, bf16[2,1024,1024]{2,1,0:T(8,128)(2,1)S(1)}, u32[]{:S(2)}) copy-start(bf16[2,1024,1024]{2,1,0:T(8,128)(2,1)S(1)} %get-tuple-element.8.proj) | copy-start | bytes 12582916
  76.2 1.4 copy-start.6
  77.6 1.0 copy-start.8
  78.6 1.0 copy-start.9
  100.8 2.2 %copy-start.2 = (bf16[2,1024,1024]{2,1,0:T(8,128)(2,1)S(1)}, bf16[2,1024,1024]{2,1,0:T(8,128)(2,1)}, u32[]{:S(2)}) copy-start(bf16[2,1024,1024]{2,1,0:T(8,128)(2,1)} %get-tuple-element.9.image) | copy-start | bytes 12582916
